TPU v7x, 32 devices: a whole 2x2x4 slice. The times are simulated.
32 devices in a mesh: pencil: 8 (over z, y), lev: 4 (over x, core).
Axes of the slice: x: 2, y: 2, z: 4, core: 2. Of those that a mesh axis runs over, the one named last changes fastest.
Arguments:
- background_std: float32 [4, 4096, 2048], P('lev', 'pencil'), may hold values from 0.4 to 6.1
- x_kernel: float32 [4, 31], P('lev'), may hold values from -0.06 to 0.12
- y_kernel: float32 [4, 31], P('lev'), may hold values from -0.06 to 0.12
- obs_owner: int32 [8192, 1], P(('pencil', 'lev')), may hold values from 0 to 7; in each aligned block of 256 rows (0 to 255, 256 to 511, ...) at most 64 rows name the same one
- obs_cells: int32 [8192, 16], P(('pencil', 'lev')), may hold values from 0 to 1048575, as said below
- obs_weights: float32 [8192, 16], P(('pencil', 'lev')), may hold values from -0.05 to 0.2
- innovation: float32 [8192], P(('pencil', 'lev')), may hold values from -6 to 6
- obs_precision: float32 [8192], P(('pencil', 'lev')), may hold values from 0.25 to 4
- obs_counts: int32 [32], P(('pencil', 'lev')), may hold values from 129 to 256, as said below
Outputs:
- control: float32 [4, 2048, 4096], P('lev', 'pencil')
- increment: float32 [4, 4096, 2048], P('lev', 'pencil')
Inputs may be any that keep to these rules, and one draw needn't show every extreme that they name: `obs_owner`: no device holds more than 64 observations of one owner, and some device reaches 64. `obs_cells`: indices into the owner's tile of 1 slabs by 512 columns by 2048 rows, flattened in that order. `obs_counts`: some device has all 256 slots live.
All inputs are finite; a program needn't handle non-finite values.
Results may differ from a plain program's by a relative error of at most 0.0001.
Values sent between devices are 32-bit elements; how exact they have to be, the bound alone decides.
No kernel may reach another device: no remote copies, remote signals or barrier semaphores. Data moves between devices by JAX's collectives and lax.ppermute only.
A program may use at most 64 MiB of HBM per device.

v0:
```python
import jax
import jax.numpy as jnp
from jax import lax
from jax.sharding import PartitionSpec as P

ITERS = 2


def smooth(grid_field, kernel_taps, periodic):
    taps = kernel_taps.shape[1]
    margin = taps // 2
    length = grid_field.shape[2]
    if periodic:
        padded = jnp.concatenate(
            [grid_field[:, :, length - margin :], grid_field, grid_field[:, :, :margin]], axis=2
        )
    else:
        padded = jnp.pad(grid_field, ((0, 0), (0, 0), (margin, margin)))
    result = jnp.zeros(grid_field.shape, jnp.float32)
    for offset in range(taps):
        result = (
            result + kernel_taps[:, offset][:, None, None] * padded[:, :, offset : offset + length]
        )
    return result


def total_squares(values):
    return lax.psum(jnp.sum(values * values), ("pencil", "lev"))


def body(
    background_std,
    x_kernel,
    y_kernel,
    obs_owner,
    obs_cells,
    obs_weights,
    innovation,
    obs_precision,
    obs_counts,
):
    pencils = lax.axis_size("pencil")
    slab_count, columns, height = background_std.shape
    holding = obs_owner.shape[0]
    stencil_size = obs_cells.shape[1]
    capacity = 2 * holding // pencils
    ordinal = jnp.arange(holding, dtype=jnp.int32)
    living = (ordinal < obs_counts[0]).astype(jnp.float32)
    target = obs_owner[:, 0]
    member = (target[:, None] == jnp.arange(pencils, dtype=jnp.int32)[None, :]).astype(jnp.int32)
    earlier = jnp.cumsum(member, axis=0) - member
    slot_index = target * capacity + jnp.sum(earlier * member, axis=1)
    packed = jnp.concatenate(
        [obs_weights, innovation[:, None], (obs_precision * living)[:, None]], axis=1
    )
    send_values = (
        jnp.zeros((pencils * capacity, packed.shape[1]), jnp.float32).at[slot_index].set(packed)
    )
    send_cells = (
        jnp.zeros((pencils * capacity, stencil_size), jnp.int32).at[slot_index].set(obs_cells)
    )
    recv_cells, recv_values = (
        lax.all_to_all(
            send_cells.reshape(pencils, capacity, stencil_size),
            "pencil",
            split_axis=0,
            concat_axis=0,
            tiled=True,
        ),
        lax.all_to_all(
            send_values.reshape(pencils, capacity, packed.shape[1]),
            "pencil",
            split_axis=0,
            concat_axis=0,
            tiled=True,
        ),
    )
    stencil = recv_cells.reshape(-1, stencil_size)
    received = recv_values.reshape(-1, packed.shape[1])
    interp = received[:, :stencil_size]
    departure = received[:, stencil_size]
    weight = received[:, stencil_size + 1]

    def spread(values):
        total = jnp.zeros((slab_count * columns * height,), jnp.float32)
        total = total.at[stencil.reshape(-1)].add((interp * values[:, None]).reshape(-1))
        return total.reshape(slab_count, columns, height)

    def adjoint(column_field):
        along_y = smooth(background_std * column_field, y_kernel[:, ::-1], False)
        turned = lax.all_to_all(
            jnp.swapaxes(along_y, 1, 2), "pencil", split_axis=1, concat_axis=2, tiled=True
        )
        return smooth(turned, x_kernel[:, ::-1], True)

    gradient_rhs = adjoint(spread(weight * departure))
    control = jnp.zeros_like(gradient_rhs)
    increment = jnp.zeros_like(background_std)
    resid = gradient_rhs
    direction = gradient_rhs
    norm_now = total_squares(resid)
    for iteration in range(ITERS):
        along_x = smooth(direction, x_kernel, True)
        forward_turned = lax.all_to_all(along_x, "pencil", split_axis=2, concat_axis=1, tiled=True)
        smoothed = background_std * smooth(jnp.swapaxes(forward_turned, 1, 2), y_kernel, False)
        image = direction + adjoint(
            spread(weight * jnp.sum(interp * smoothed.reshape(-1)[stencil], axis=1))
        )
        step_length = norm_now / lax.psum(jnp.sum(direction * image), ("pencil", "lev"))
        control = control + step_length * direction
        increment = increment + step_length * smoothed
        resid = resid - step_length * image
        norm_next = total_squares(resid)
        direction = resid + norm_next / norm_now * direction
        norm_now = norm_next
    return (control, increment)


def solution(mesh):
    return jax.shard_map(
        body,
        mesh=mesh,
        in_specs=(
            P("lev", "pencil", None),
            P("lev", None),
            P("lev", None),
            P(("pencil", "lev"), None),
            P(("pencil", "lev"), None),
            P(("pencil", "lev"), None),
            P(("pencil", "lev")),
            P(("pencil", "lev")),
            P(("pencil", "lev")),
        ),
        out_specs=(P("lev", "pencil", None), P("lev", "pencil", None)),
        check_vma=False,
    )
```

profile of v0, /device:TPU:0, one launch (start us, length us, event | category | flops | bytes accessed | tf_op | source)
XLA Modules:
  0.0 2379.1 jit_solution(17279320075474146601)
XLA Ops:
  6.5 7.3 all-to-all-start
  36.7 48.8 %scatter_custom_fusion.2 = f32[1048576]{0:T(1024)} fusion(s32[8192]{0:T(1024)S(1)} %bitcast.169, f32[8192]{0:T(1024)S(1)} %reshape.572, f32[]{:T(128)} %constant.5.clone.1), kind=kCustom, calls=%fused_computation.941 | custom fusion | flops 8192 | bytes 4194308 | tf_op jit(solution)/shard_map/scatter-add | solution.py:86
  94.7 53.2 %add_bitcast_fusion.2 = f32[1,2048,512]{1,2,0:T(8,128)} fusion(f32[1,512,2048]{2,1,0:T(8,128)S(1)} %mul.984, f32[]{:T(128)} %bitcast.44, f32[]{:T(128)} %bitcast.43, f32[]{:T(128)} %bitcast.42, f32[]{:T(128)} %bitcast.41, f32[]{:T(128)} %bitcast.40, f32[]{:T(128)} %bitcast.39, f32[]{:T(128)} %bitcast.38, f32[]{:T(128)} %bitcast.37, f32[]{:T(128)} %bitcast.36, ...), kind=kLoop, calls=%fused_computation.895 | loop fusion | flops 63963136 | bytes 8388732 | tf_op jit(solution)/shard_map/transpose | solution.py:92
  147.9 10.9 copy.599
  158.8 8.7 all-to-all-start.2
  169.0 90.5 %all-to-all-done.2 = f32[1,2048,512]{2,0,1:T(1,128)} async-done(((f32[1,2048,512]{2,0,1:T(1,128)}), f32[1,2048,512]{2,0,1:T(1,128)}, u32[]{:S(2)}, u32[]{:S(2)}) %all-to-all-start.2) | async-done | bytes 4194336 | tf_op jit(solution)/shard_map/all_to_all | solution.py:91
  259.5 6.6 copy.624
  272.1 105.3 %fusion.349 = f32[1,256,4096]{2,1,0:T(8,128)S(1)} fusion(f32[1,256,15]{2,1,0:T(8,128)S(1)} %get-tuple-element.22, f32[1,256,15]{2,1,0:T(8,128)S(1)} %get-tuple-element.21, f32[1,256,4096]{2,1,0:T(8,128)} %all_to_all.76, f32[]{:T(128)} %bitcast.77, f32[]{:T(128)} %bitcast.76, f32[]{:T(128)} %bitcast.75, f32[]{:T(128)} %bitcast.74, f32[]{:T(128)} %bitcast.73, ...), kind=kLoop, calls=%fused_computation.497 | loop fusion | flops 95420416 | bytes 8419452 | tf_op jit(solution)/shard_map/add | solution.py:22
  379.5 62.5 %fusion.263 = f32[1,256,4096]{2,1,0:T(8,128)} fusion(f32[1,256,15]{2,1,0:T(8,128)S(1)} %get-tuple-element.20, f32[1,256,15]{2,1,0:T(8,128)S(1)} %get-tuple-element.19, f32[1,256,4096]{2,1,0:T(8,128)S(1)} %fusion.349, f32[]{:T(128)} %bitcast.77, f32[]{:T(128)} %bitcast.76, f32[]{:T(128)} %bitcast.75, f32[]{:T(128)} %bitcast.74, f32[]{:T(128)} %bitcast.73, ...), kind=kLoop, calls=%fused_computation.411 | loop fusion | flops 95420416 | bytes 8419452 | tf_op jit(solution)/shard_map/add | solution.py:22
  442.0 10.2 copy.601
  457.6 92.2 %all-to-all-done.3 = f32[1,256,4096]{1,0,2:T(1,128)} async-done(((f32[1,256,4096]{1,0,2:T(1,128)}), f32[1,256,4096]{1,0,2:T(1,128)}, u32[]{:S(2)}, u32[]{:S(2)}) %all-to-all-start.3) | async-done | bytes 4194336 | tf_op jit(solution)/shard_map/all_to_all | solution.py:104
  561.3 97.3 %add_multiply_fusion.2 = f32[1,512,2048]{2,1,0:T(8,128)S(1)} fusion(f32[1,512,2048]{2,1,0:T(8,128)} %param.9, f32[1,512,2048]{2,1,0:T(8,128)} %bitcast.152, f32[]{:T(128)} %bitcast.44, f32[]{:T(128)} %bitcast.43, f32[]{:T(128)} %bitcast.42, f32[]{:T(128)} %bitcast.41, f32[]{:T(128)} %bitcast.40, f32[]{:T(128)} %bitcast.39, f32[]{:T(128)} %bitcast.38, ...), kind=kLoop, calls=%fused_computation.852 | loop fusion | flops 65011712 | bytes 12583036 | tf_op jit(solution)/shard_map/mul | solution.py:105
  661.9 173.9 %gather_fusion = f32[8192]{0:T(1024)S(1)} fusion(f32[1048576]{0:T(1024)} %bitcast.141, s32[8192]{0:T(1024)S(1)} %broadcast_clamp_fusion), kind=kCustom, calls=%fused_computation | custom fusion | bytes 98304 | tf_op jit(solution)/shard_map/gather | solution.py:107
  836.7 49.0 %scatter_custom_fusion.3 = f32[1048576]{0:T(1024)} fusion(s32[8192]{0:T(1024)S(1)} %bitcast.170, f32[8192]{0:T(1024)S(1)} %reshape.580, f32[]{:T(128)} %constant.5.clone.1), kind=kCustom, calls=%fused_computation.939 | custom fusion | flops 8192 | bytes 4194308 | tf_op jit(solution)/shard_map/scatter-add | solution.py:86
  894.9 53.2 %add_bitcast_fusion.1 = f32[1,2048,512]{1,2,0:T(8,128)} fusion(f32[1,512,2048]{2,1,0:T(8,128)S(1)} %mul.1236, f32[]{:T(128)} %bitcast.44, f32[]{:T(128)} %bitcast.43, f32[]{:T(128)} %bitcast.42, f32[]{:T(128)} %bitcast.41, f32[]{:T(128)} %bitcast.40, f32[]{:T(128)} %bitcast.39, f32[]{:T(128)} %bitcast.38, f32[]{:T(128)} %bitcast.37, f32[]{:T(128)} %bitcast.36, ...), kind=kLoop, calls=%fused_computation.810 | loop fusion | flops 63963136 | bytes 8388732 | tf_op jit(solution)/shard_map/transpose | solution.py:92
  948.1 10.9 copy.606
  959.0 212.7 %all_to_all.100 = f32[1,2048,512]{2,0,1:T(1,128)S(1)} all-to-all(f32[1,2048,512]{2,0,1:T(1,128)} %copy.606), channel_id=1, replica_groups=mesh['pencil'=8,'lev'=4] {'pencil'}, dimensions={1} | all-to-all | bytes 8388608 | tf_op jit(solution)/shard_map/all_to_all | solution.py:91
  1182.2 107.4 %multiply_reduce_fusion.1 = (f32[]{:T(128)}, f32[]{:T(128)}, f32[1,256,4096]{2,1,0:T(8,128)}) fusion(f32[1,256,4096]{2,1,0:T(8,128)} %copy-done, f32[1,256,15]{2,1,0:T(8,128)S(1)} %get-tuple-element.18, f32[1,256,4096]{2,1,0:T(8,128)} %all_to_all.84, f32[]{:T(128)} %bitcast.77, f32[]{:T(128)} %bitcast.76, f32[]{:T(128)} %bitcast.75, f32[]{:T(128)} %bitcast.74, ...), kind=kLoop, calls=%fused_computation.809 | loop fusion | flops 100663296 | bytes 12613764 | tf_op jit(solution)/shard_map/reduce_sum | solution.py:109
  1289.5 58.5 %all-reduce.5 = (f32[]{:T(128)}, f32[]{:T(128)}) all-reduce(f32[]{:T(128)} %get-tuple-element.9, f32[]{:T(128)} %get-tuple-element.8), channel_id=1, replica_groups=mesh['pencil'=8,'lev'=4] {'pencil','lev'}, use_global_device_ids=true, to_apply=%region_7.8 | all-reduce | flops 2 | bytes 16 | tf_op jit(solution)/shard_map/psum | solution.py:28
  1354.6 41.2 %psum.30 = f32[]{:T(128)} all-reduce(f32[]{:T(128)} %multiply_reduce_fusion), channel_id=1, replica_groups=mesh['pencil'=8,'lev'=4] {'pencil','lev'}, use_global_device_ids=true, to_apply=%region_13.14 | all-reduce | flops 1 | bytes 8 | tf_op jit(solution)/shard_map/psum | solution.py:28
  1403.3 62.5 %fusion.90 = f32[1,256,4096]{2,1,0:T(8,128)} fusion(f32[1,256,15]{2,1,0:T(8,128)S(1)} %get-tuple-element.16, f32[1,256,15]{2,1,0:T(8,128)S(1)} %get-tuple-element.15, f32[1,256,4096]{2,1,0:T(8,128)S(1)} %multiply_add_fusion.2, f32[]{:T(128)} %bitcast.77, f32[]{:T(128)} %bitcast.76, f32[]{:T(128)} %bitcast.75, f32[]{:T(128)} %bitcast.74, f32[]{:T(128)} %bitcast.73, ...), kind=kLoop, calls=%fused_computation.238 | loop fusion | flops 95420416 | bytes 8419452 | tf_op jit(solution)/shard_map/add | solution.py:22
  1465.8 10.2 copy.608
  1476.0 96.5 %all_to_all.101 = f32[1,256,4096]{1,0,2:T(1,128)S(1)} all-to-all(f32[1,256,4096]{1,0,2:T(1,128)} %copy.608), channel_id=1, replica_groups=mesh['pencil'=8,'lev'=4] {'pencil'}, dimensions={2} | all-to-all | bytes 8388608 | tf_op jit(solution)/shard_map/all_to_all | solution.py:104
  1581.8 98.5 %add_multiply_fusion.1 = f32[1,512,2048]{2,1,0:T(8,128)S(1)} fusion(f32[1,512,2048]{2,1,0:T(8,128)} %param.9, f32[1,512,2048]{2,1,0:T(8,128)} %bitcast.153, f32[]{:T(128)} %bitcast.44, f32[]{:T(128)} %bitcast.43, f32[]{:T(128)} %bitcast.42, f32[]{:T(128)} %bitcast.41, f32[]{:T(128)} %bitcast.40, f32[]{:T(128)} %bitcast.39, f32[]{:T(128)} %bitcast.38, ...), kind=kLoop, calls=%fused_computation.764 | loop fusion | flops 65011712 | bytes 12583036 | tf_op jit(solution)/shard_map/mul | solution.py:105
  1683.8 173.9 %gather_fusion.1 = f32[8192]{0:T(1024)S(1)} fusion(f32[1048576]{0:T(1024)} %bitcast.140, s32[8192]{0:T(1024)S(1)} %broadcast_clamp_fusion), kind=kCustom, calls=%fused_computation.1 | custom fusion | bytes 98304 | tf_op jit(solution)/shard_map/gather | solution.py:107
  1858.6 49.0 %scatter_custom_fusion.4 = f32[1048576]{0:T(1024)} fusion(s32[8192]{0:T(1024)S(1)} %bitcast.171, f32[8192]{0:T(1024)S(1)} %reshape.588, f32[]{:T(128)} %constant.5.clone.1), kind=kCustom, calls=%fused_computation.937 | custom fusion | flops 8192 | bytes 4194308 | tf_op jit(solution)/shard_map/scatter-add | solution.py:86
  1916.7 53.2 %add_bitcast_fusion = f32[1,2048,512]{1,2,0:T(8,128)} fusion(f32[1,512,2048]{2,1,0:T(8,128)S(1)} %mul.2656, f32[]{:T(128)} %bitcast.44, f32[]{:T(128)} %bitcast.43, f32[]{:T(128)} %bitcast.42, f32[]{:T(128)} %bitcast.41, f32[]{:T(128)} %bitcast.40, f32[]{:T(128)} %bitcast.39, f32[]{:T(128)} %bitcast.38, f32[]{:T(128)} %bitcast.37, f32[]{:T(128)} %bitcast.36, ...), kind=kLoop, calls=%fused_computation.722 | loop fusion | flops 63963136 | bytes 8388732 | tf_op jit(solution)/shard_map/transpose | solution.py:92
  1969.9 10.9 copy.611
  1980.8 211.4 %all_to_all.102 = f32[1,2048,512]{2,0,1:T(1,128)S(1)} all-to-all(f32[1,2048,512]{2,0,1:T(1,128)} %copy.611), channel_id=1, replica_groups=mesh['pencil'=8,'lev'=4] {'pencil'}, dimensions={1} | all-to-all | bytes 8388608 | tf_op jit(solution)/shard_map/all_to_all | solution.py:91
  2202.7 107.5 %fusion = f32[]{:T(128)} fusion(f32[1,256,4096]{2,1,0:T(8,128)} %copy-done.2, f32[1,256,15]{2,1,0:T(8,128)S(1)} %get-tuple-element.14, f32[1,256,15]{2,1,0:T(8,128)S(1)} %get-tuple-element.13, f32[1,256,4096]{2,1,0:T(8,128)} %all_to_all.92, f32[]{:T(128)} %bitcast.77, f32[]{:T(128)} %bitcast.76, f32[]{:T(128)} %bitcast.75, f32[]{:T(128)} %bitcast.74, ...), kind=kLoop, calls=%fused_computation.148 | loop fusion | flops 98566144 | bytes 8419456 | tf_op jit(solution)/shard_map/reduce_sum | solution.py:109
  2310.2 57.7 %psum.31 = f32[]{:T(128)} all-reduce(f32[]{:T(128)} %fusion), channel_id=1, replica_groups=mesh['pencil'=8,'lev'=4] {'pencil','lev'}, use_global_device_ids=true, to_apply=%region_17.18 | all-reduce | flops 1 | bytes 8 | tf_op jit(solution)/shard_map/psum | solution.py:109
  2369.3 6.9 multiply_add_fusion
  (95 shorter events, 134.7 us)
Async XLA Ops:
  6.5 15.5 all-to-all-start
  21.9 12.7 all-to-all-start.1
  158.8 8.7 copy-start.6
  158.8 100.7 %all-to-all-start.2 = ((f32[1,2048,512]{2,0,1:T(1,128)}), f32[1,2048,512]{2,0,1:T(1,128)}, u32[]{:S(2)}, u32[]{:S(2)}) async-start(f32[1,2048,512]{2,0,1:T(1,128)} %copy.599), calls=%async_computation.2 | async-start | bytes 8388608 | tf_op jit(solution)/shard_map/all_to_all | solution.py:91
  377.5 2.0 copy-start
  452.2 97.5 %all-to-all-start.3 = ((f32[1,256,4096]{1,0,2:T(1,128)}), f32[1,256,4096]{1,0,2:T(1,128)}, u32[]{:S(2)}, u32[]{:S(2)}) async-start(f32[1,256,4096]{1,0,2:T(1,128)} %copy.601), calls=%async_computation.3 | async-start | bytes 8388608 | tf_op jit(solution)/shard_map/all_to_all | solution.py:104
  658.5 3.4 copy-start.4
  1401.3 2.0 copy-start.2
  1680.4 3.4 copy-start.5
  2369.3 6.9 copy-start.1
  2369.3 6.9 copy-start.3
where the time goes:
time: 2400 us; the launch traced here: 2380 us
  other arithmetic  986 us (41%)
  blocking collectives  678 us (28%)
  local copies, waits for them, and re-layouts  494 us (21%)
  waiting for transfers between devices  188 us (8%)
  starting transfers between devices  27 us (1%)
    all_to_all x2, blocking collectives, adjoint(): lax.all_to_all(jnp.swapaxes(along_y, 1, 2), 'pencil', split_axis=1, conca...  424 us
    gather x4, local copies, waits for them, and re-layouts, body(): smoothed.reshape(-1)[stencil]  348 us
    add x3, other arithmetic, smooth(): result + kernel_taps[:, offset][:, None, None] * padded[:, :, offset:offs...  230 us
    reduce_sum x2, other arithmetic, body(): jnp.sum(direction * image)  215 us
    mul x2, other arithmetic, body(): background_std * smooth(jnp.swapaxes(forward_turned, 1, 2), y_kernel, False)  196 us
    transpose x3, other arithmetic, adjoint(): jnp.swapaxes(along_y, 1, 2)  160 us
    scatter-add x3, other arithmetic, spread(): total.at[stencil.reshape(-1)].add((interp * values[:, None]).reshape(-1))  147 us
    psum x2, blocking collectives, total_squares(): return lax.psum(jnp.sum(values * values), ('pencil', 'lev'))  99.7 us
  transfers between devices with their start and end apart: 4, of which 3 were waited for; matrix products, arithmetic and copies ran while one was open for 0% of the time, Pallas kernels for 0%

commit v1 on v0

v1 whole, which is shorter than its diff:
```python
import functools

import jax
import jax.numpy as jnp
import numpy as np
from jax import lax
from jax.experimental import pallas as pl
from jax.experimental.pallas import tpu as pltpu
from jax.sharding import PartitionSpec as P


BF = jnp.bfloat16
F32 = jnp.float32
I32 = jnp.int32
LANES = 128
WIDE = 256
HALO = 32
PAD = 16
PACK = 40
INFO = 24
GROUP = 8
COPIES = 4
VMEM_LIMIT = 58 * 1024 * 1024


def vmem():
    return pl.BlockSpec(memory_space=pltpu.VMEM)


def smem():
    return pl.BlockSpec(memory_space=pltpu.SMEM)


def hbm():
    return pl.BlockSpec(memory_space=pl.ANY)


def params():
    return pltpu.CompilerParams(vmem_limit_bytes=VMEM_LIMIT)


def split2(x):
    high = x.astype(BF)
    return high, (x - high.astype(F32)).astype(BF)


def split3(x):
    high = x.astype(BF)
    rest = x - high.astype(F32)
    mid = rest.astype(BF)
    return high, mid, (rest - mid.astype(F32)).astype(BF)


def mm(a, b):
    return jnp.dot(a, b, preferred_element_type=F32)


def mm_parts(a_parts, b_parts):
    (ah, al), (bh, bl) = a_parts, b_parts
    return mm(ah, bh) + (mm(al, bh) + mm(ah, bl))


def iota(shape, dim):
    return lax.broadcasted_iota(I32, shape, dim)


def pack_kernel(counts, owner, cells, weights, extra, out, *, parts, columns, height, margin):
    hold = owner.shape[0]
    shift = height.bit_length() - 1
    block = height // parts
    reach = 2 * margin
    row_id = iota((hold, hold), 0)
    col_id = iota((hold, hold), 1)
    eye = row_id == col_id
    col_f = col_id.astype(F32)
    live = iota((hold, 1), 0) < counts[0]
    cell = cells[...]
    column = lax.shift_right_logical(cell, jnp.full(cell.shape, shift, I32))
    row = cell & (height - 1)

    def any_of(mask):
        return jnp.max(jnp.where(mask, 1.0, 0.0), axis=1, keepdims=True)

    left = any_of(column < reach)
    right = any_of(column >= columns - reach)
    side = left + 3.0 * right - 2.0 * left * right
    key = jnp.where(live, owner[...].astype(F32) * 4.0 + side, 4.0 * parts)
    key_row = jnp.sum(jnp.where(eye, key, 0.0), axis=0, keepdims=True)
    before = (key_row < key) | ((key_row == key) & (col_id < row_id))
    rank = jnp.sum(jnp.where(before, 1.0, 0.0), axis=1, keepdims=True)
    perm = jnp.where(rank == col_f, 1.0, 0.0).astype(BF)

    def sort_cols(values):
        total = None
        for part in split3(values):
            term = lax.dot_general(
                part, perm, (((0,), (0,)), ((), ())), preferred_element_type=F32
            )
            total = term if total is None else total + term
        return total

    def sort_rows(values):
        total = None
        for part in split3(values):
            term = mm(part, perm)
            total = term if total is None else total + term
        return total

    sorted_cells = sort_cols(cell.astype(F32))
    sorted_weights = sort_cols(weights[...])
    rest = jnp.concatenate([extra[0:2, :], key_row, jnp.zeros((5, hold), F32)], axis=0)
    rest = sort_rows(rest)
    line = iota((8, hold), 0)
    stencil = cells.shape[1]

    def per_part(part, carry):
        low = part * block - margin
        high = (part + 1) * block + margin
        flag = jnp.where(live, any_of((row >= low) & (row < high)), 0.0)
        flag_row = jnp.sum(jnp.where(eye, flag, 0.0), axis=0, keepdims=True)
        place = jnp.sum(jnp.where(col_id < row_id, flag_row, 0.0), axis=1, keepdims=True)
        chosen = (place == col_f) & (flag > 0.0)
        listed = jnp.sum(jnp.where(chosen, rank, 0.0), axis=0, keepdims=True)
        amount = jnp.sum(flag_row, axis=1, keepdims=True)
        tail = jnp.where(line == 3, listed, jnp.where(line == 4, amount, rest))
        out[part, 0:stencil, :] = sorted_cells
        out[part, stencil : 2 * stencil, :] = sorted_weights
        out[part, 2 * stencil : 2 * stencil + 8, :] = tail
        return carry

    lax.fori_loop(0, parts, per_part, 0)


def band(shape, taps, shift):
    distance = iota(shape, 1) - iota(shape, 0) + shift
    result = jnp.zeros(shape, F32)
    for tap in range(taps.shape[0]):
        result = jnp.where(distance == tap, taps[tap], result)
    return result


def band_rev(shape, taps, shift):
    distance = iota(shape, 0) - iota(shape, 1) + shift
    result = jnp.zeros(shape, F32)
    for tap in range(taps.shape[0]):
        result = jnp.where(distance == tap, taps[tap], result)
    return result


def exact_nt(a, b):
    return lax.dot_general(
        a,
        b,
        (((1,), (1,)), ((), ())),
        precision=lax.Precision.HIGHEST,
        preferred_element_type=F32,
    )


def store_split(ref, index, value):
    high, low = split2(value)
    ref[(0,) + index] = high
    ref[(1,) + index] = low


def bands_kernel(kx, ky, lat2, lon2, lat1, lon1, *, rows_block):
    margin = kx.shape[0] // 2
    window = lat2.shape[2]
    first = band((window, window), ky, margin)
    reach = first[LANES : LANES + WIDE, :]
    place = iota((window, window), 1)
    for variant in range(3):
        kept = first
        if variant == 0:
            kept = jnp.where(place >= LANES, first, 0.0)
        if variant == 2:
            kept = jnp.where(place < LANES + WIDE, first, 0.0)
        store_split(lat2, (variant,), exact_nt(kept, reach))
    size = lon2.shape[1]
    wide = size + 2 * HALO
    depth = (wide + 32 + LANES - 1) // LANES * LANES
    second = band((wide, depth), kx, -(16 - margin))
    store_split(lon2, (), exact_nt(second[HALO : HALO + size, :], second))
    store_split(lat1, (), band_rev((rows_block, rows_block + 2 * PAD), ky, PAD + margin))
    store_split(lon1, (), band((2 * WIDE, WIDE), kx, LANES + margin))


def for_each(sender_count, ranges, action):
    def per_sender(sender, carry):
        for low, high, tag in ranges(sender):

            def step(idx, inner, sender=sender, tag=tag):
                action(sender, idx, tag)
                return inner

            lax.fori_loop(low, high, step, 0)
        return carry

    lax.fori_loop(0, sender_count, per_sender, 0)


def zero_all(refs):
    rows = refs[0].shape[0]
    step = 256

    def clear(i, carry):
        for ref in refs:
            ref[pl.ds(pl.multiple_of(i * step, 8), step), :] = jnp.zeros((step, LANES), F32)
        return carry

    whole = rows // step
    lax.fori_loop(0, whole, clear, 0)
    if rows % step:
        for ref in refs:
            ref[whole * step : rows, :] = jnp.zeros((rows % step, LANES), F32)


def scatter_entries(copies, entry, lane, stencil):
    for start in range(0, stencil, len(copies)):
        group = []
        for j in range(min(len(copies), stencil - start)):
            address, value = entry(start + j)
            line = lax.shift_right_logical(address, 7)
            spread = jnp.where(lane == (address & (LANES - 1)), value, 0.0)
            group.append((copies[j], line, copies[j][pl.ds(line, 1), :] + spread))
        for ref, line, value in group:
            ref[pl.ds(line, 1), :] = value


def apply_kernel(
    *refs, first, columns, height, hold, stencil, capacity, senders, parts, table
):
    refs = list(refs)
    meta, addr_h, wgt_h, val_h, start_h = refs[:5]
    del refs[:5]
    if first:
        prec_h = refs.pop(0)
    std, std_l, std_r, lat2, lon2 = refs[:5]
    field, info = refs[5:7]
    del refs[:7]
    if first:
        column_info = refs.pop(0)
    addr, wgt, val, start = refs[:4]
    del refs[:4]
    if first:
        prec, std_flat, reply = refs[:3]
        del refs[:3]
    sums, high_s, low_s = refs[:3]
    del refs[:3]
    copies = refs[:COPIES]
    sems = refs[COPIES]

    me = meta[0]
    wide = columns + 2 * HALO
    blocks = height // LANES
    group = min(GROUP, senders)
    chunks = senders // group
    slots = senders * capacity
    lane = iota((1, LANES), 1)
    per = stencil * hold

    def chunk_copies(chunk):
        todo = [(addr_h, addr, group * per), (wgt_h, wgt, group * per)]
        todo.append((start_h, start, group * table))
        if first:
            todo.append((val_h, val, group * hold))
            todo.append((prec_h, prec, group * hold))
        result = []
        for i, (source, target, size) in enumerate(todo):
            part = source if chunks == 1 else source.at[pl.ds(chunk * size, size)]
            result.append(pltpu.make_async_copy(part, target, sems.at[i]))
        return result

    def load_chunk(chunk):
        for copy in chunk_copies(chunk):
            copy.start()
        for copy in chunk_copies(chunk):
            copy.wait()

    if not first:
        whole = pltpu.make_async_copy(val_h, val, sems.at[3])
        whole.start()
    if chunks == 1:
        pending = chunk_copies(0)
        for copy in pending:
            copy.start()
    zero_all(copies)
    zero_all([sums] + ([reply] if first else []))
    if chunks == 1:
        for copy in pending:
            copy.wait()
    if not first:
        whole.wait()

    after = lax.rem(me + 1, parts)
    ahead = lax.rem(me + parts - 1, parts)

    def start_of(sender, key):
        return start[sender * table + key]

    def scatter_chunk(chunk):
        def ranges(sender):
            for owner, low, high in ((me, 0, 4), (after, 1, 3), (ahead, 2, 4)):
                yield start_of(sender, owner * 4 + low), start_of(sender, owner * 4 + high), owner

        def action(sender, idx, owner):
            if first:
                value = val[sender * hold + idx]
            else:
                place = idx - start_of(sender, owner * 4)
                value = val[owner * slots + (chunk * group + sender) * capacity + place]
            base = sender * per + idx

            def entry(k):
                at = base + k * hold
                return addr[at], wgt[at] * value

            scatter_entries(copies, entry, lane, stencil)

        for_each(group, ranges, action)

    def over_chunks(work):
        if chunks == 1:
            work(0)
        else:

            def step(chunk, carry):
                load_chunk(chunk)
                work(chunk)
                return carry

            lax.fori_loop(0, chunks, step, 0)

    over_chunks(scatter_chunk)

    for jb in range(blocks):
        lanes = slice(jb * LANES, (jb + 1) * LANES)
        for low, size, source, at in (
            (0, HALO, std_l, 0),
            (HALO, columns, std, 0),
            (HALO + columns, HALO, std_r, 0),
        ):
            rows = slice(jb * wide + low, jb * wide + low + size)
            total = copies[0][rows, :]
            for ref in copies[1:]:
                total = total + ref[rows, :]
            high, lo = split2(total * source[:, lanes])
            high_s[low : low + size, lanes] = high
            low_s[low : low + size, lanes] = lo
        if first:
            std_flat[jb * wide + HALO : jb * wide + HALO + columns, :] = std[:, lanes]

    smoothed = copies[0]
    size = lon2.shape[1]
    count = height // WIDE
    for block in range(count):
        variant = 0 if block == 0 else (2 if block == count - 1 else 1)
        low = max(block * WIDE - LANES, 0)
        high = min(block * WIDE + WIDE + LANES, height)
        inner = slice(low - (block * WIDE - LANES), high - (block * WIDE - LANES))
        matrix = (lat2[0, variant, inner, :], lat2[1, variant, inner, :])
        along = mm_parts((high_s[:, low:high], low_s[:, low:high]), matrix)
        parts_y = split2(along)
        lanes = slice(block * WIDE, (block + 1) * WIDE)
        for part in range(columns // size):
            rows = slice(part * size, (part + 1) * size)
            window = slice(part * size, part * size + size + 2 * HALO)
            result = mm_parts(
                (lon2[0], lon2[1]), (parts_y[0][window, :], parts_y[1][window, :])
            )
            field[rows, lanes] = result
            scaled = result * std[rows, lanes]
            for half in range(WIDE // LANES):
                top = (block * (WIDE // LANES) + half) * wide + HALO + part * size
                smoothed[top : top + size, :] = scaled[:, half * LANES : (half + 1) * LANES]

    def gather_chunk(chunk):
        def ranges(sender):
            yield start_of(sender, me * 4), start_of(sender, me * 4 + 4), 0

        def action(sender, idx, tag):
            slot = (chunk * group + sender) * capacity + idx - start_of(sender, me * 4)
            base = sender * per + idx
            total = jnp.zeros((1, LANES), F32)
            factors = jnp.zeros((1, LANES), F32)
            for k in range(stencil):
                at = base + k * hold
                address = addr[at]
                weight = wgt[at]
                line = lax.shift_right_logical(address, 7)
                here = address & (LANES - 1)
                mask = lane == here
                total = total + jnp.where(mask, smoothed[pl.ds(line, 1), :] * weight, 0.0)
                if first:
                    picked = jnp.where(mask, std_flat[pl.ds(line, 1), :] * weight, 0.0)
                    move = lax.rem(k - here + LANES, LANES)
                    factors = factors + pltpu.roll(picked, move, 1)
            sums[pl.ds(slot, 1), :] = total
            if first:
                factors = jnp.where(lane == stencil, prec[sender * hold + idx], factors)
                factors = jnp.where(lane == stencil + 1, val[sender * hold + idx], factors)
                reply[pl.ds(slot, 1), :] = factors

        for_each(group, ranges, action)

    over_chunks(gather_chunk)

    total = jnp.sum(sums[...], axis=1, keepdims=True)
    lanes = iota((sums.shape[0], LANES), 1)
    if first:
        factors = reply[...]
        weight = jnp.sum(jnp.where(lanes == stencil, factors, 0.0), axis=1, keepdims=True)
        source = jnp.sum(jnp.where(lanes == stencil + 1, factors, 0.0), axis=1, keepdims=True)
        back = weight * total
        factors = jnp.where(lanes == stencil + 2, back, factors)
        factors = jnp.where(lanes == stencil + 3, total, factors)
        info[...] = factors.T[0:INFO, :]
        column_info[...] = jnp.where(
            iota(column_info.shape, 1) == 0,
            jnp.sum(source * total, axis=0, keepdims=True),
            jnp.sum(back * total, axis=0, keepdims=True),
        )
    else:
        info[...] = jnp.where(lanes == 0, total, 0.0).T[0:8, :]


def final_kernel(
    coef,
    addr_h,
    list_h,
    count_h,
    slot_h,
    reply_h,
    std,
    field0,
    field1,
    lat1,
    lon1,
    control,
    increment,
    addr,
    listed,
    amount,
    slot,
    reply,
    high_s,
    low_s,
    *rest,
    hold,
    stencil,
    capacity,
    senders,
    parts,
    length,
):
    copies = rest[:COPIES]
    sems = rest[COPIES]
    group = min(GROUP, senders)
    chunks = senders // group
    per = stencil * hold
    rows_block = control.shape[0]
    high_rows = rows_block + 2 * PAD
    lane = iota((1, LANES), 1)
    size_reply = parts * INFO * group * capacity
    stride = group * capacity

    def chunk_copies(chunk):
        todo = [
            (addr_h, addr, group * per),
            (list_h, listed, group * hold),
            (count_h, amount, group * LANES),
            (slot_h, slot, group * hold),
            (reply_h, reply, size_reply),
        ]
        result = []
        for i, (source, target, size) in enumerate(todo):
            part = source if chunks == 1 else source.at[pl.ds(chunk * size, size)]
            result.append(pltpu.make_async_copy(part, target, sems.at[i]))
        return result

    if chunks == 1:
        pending = chunk_copies(0)
        for copy in pending:
            copy.start()
    zero_all(copies)
    first, second = coef[0], coef[1]
    increment[...] = std[...] * (first * field0[...] + second * field1[...])

    def scatter_chunk():
        def ranges(sender):
            yield 0, amount[sender * LANES], 0

        def action(sender, at, tag):
            idx = listed[sender * hold + at]
            place = slot[sender * hold + idx]
            base = sender * per + idx
            value = (
                first * reply[place + (stencil + 1) * stride]
                + second * reply[place + (stencil + 2) * stride]
            )

            def entry(k):
                return addr[base + k * hold], reply[place + k * stride] * value

            scatter_entries(copies, entry, lane, stencil)

        for_each(group, ranges, action)

    if chunks == 1:
        for copy in pending:
            copy.wait()
        scatter_chunk()
    else:

        def step(chunk, carry):
            for copy in chunk_copies(chunk):
                copy.start()
            for copy in chunk_copies(chunk):
                copy.wait()
            scatter_chunk()
            return carry

        lax.fori_loop(0, chunks, step, 0)

    pair = WIDE // LANES
    count = length // WIDE
    for block in range(count):
        pieces = []
        for half in range(pair):
            rows = slice((block * pair + half) * high_rows, (block * pair + half + 1) * high_rows)
            total = copies[0][rows, :]
            for ref in copies[1:]:
                total = total + ref[rows, :]
            pieces.append(total)
        along = mm_parts((lat1[0], lat1[1]), split2(jnp.concatenate(pieces, axis=1)))
        high, low = split2(along)
        high_s[:, block * WIDE : (block + 1) * WIDE] = high
        low_s[:, block * WIDE : (block + 1) * WIDE] = low

    def window(ref, block):
        low, high = block * WIDE - LANES, (block + 1) * WIDE + LANES
        if low < 0:
            return jnp.concatenate([ref[:, length + low : length], ref[:, 0:high]], axis=1)
        if high > length:
            return jnp.concatenate([ref[:, low:length], ref[:, 0 : high - length]], axis=1)
        return ref[:, low:high]

    for block in range(count):
        control[:, block * WIDE : (block + 1) * WIDE] = mm_parts(
            (window(high_s, block), window(low_s, block)), (lon1[0], lon1[1])
        )


def body(
    background_std,
    x_kernel,
    y_kernel,
    obs_owner,
    obs_cells,
    obs_weights,
    innovation,
    obs_precision,
    obs_counts,
):
    parts = lax.axis_size("pencil")
    levels = lax.axis_size("lev")
    me = lax.axis_index("pencil")
    _, columns, height = background_std.shape
    hold, stencil = obs_cells.shape
    taps = x_kernel.shape[1]
    margin = taps // 2
    capacity = 2 * hold // parts
    senders = parts
    slots = senders * capacity
    rows_block = height // parts
    length = columns * parts
    blocks = height // LANES
    wide = columns + 2 * HALO
    table = (4 * parts + 1 + LANES - 1) // LANES * LANES
    group = min(GROUP, senders)
    chunks = senders // group
    std = background_std[0]

    right = [(p, (p + 1) % parts) for p in range(parts)]
    left = [(p, (p - 1) % parts) for p in range(parts)]
    std_l = lax.ppermute(std[columns - HALO :, :], "pencil", right)
    std_r = lax.ppermute(std[:HALO, :], "pencil", left)

    packed = pl.pallas_call(
        functools.partial(
            pack_kernel, parts=parts, columns=columns, height=height, margin=margin
        ),
        out_shape=jax.ShapeDtypeStruct((parts, PACK, hold), F32),
        in_specs=[smem(), vmem(), vmem(), vmem(), vmem()],
        out_specs=vmem(),
        compiler_params=params(),
        name="pack",
    )(
        obs_counts,
        obs_owner,
        obs_cells,
        obs_weights,
        jnp.concatenate([innovation[None, :], obs_precision[None, :]], axis=0),
    )
    recv = lax.all_to_all(packed, "pencil", split_axis=0, concat_axis=0, tiled=True)

    size = min(columns, WIDE)
    lat2, lon2, lat1, lon1 = pl.pallas_call(
        functools.partial(bands_kernel, rows_block=rows_block),
        out_shape=[
            jax.ShapeDtypeStruct((2, 3, 2 * WIDE, WIDE), BF),
            jax.ShapeDtypeStruct((2, size, size + 2 * HALO), BF),
            jax.ShapeDtypeStruct((2, rows_block, rows_block + 2 * PAD), BF),
            jax.ShapeDtypeStruct((2, 2 * WIDE, WIDE), BF),
        ],
        in_specs=[smem(), smem()],
        out_specs=[vmem()] * 4,
        compiler_params=params(),
        name="bands",
    )(x_kernel[0], y_kernel[0])

    cell = recv[:, :stencil, :].astype(I32)
    weights = recv[:, stencil : 2 * stencil, :]
    precision = recv[:, 2 * stencil + 1, :]
    source = precision * recv[:, 2 * stencil, :]
    key = recv[:, 2 * stencil + 2, :].astype(I32)
    listed = recv[:, 2 * stencil + 3, :].astype(I32)
    amount = recv[:, 2 * stencil + 4, :LANES].astype(I32)
    owner = key // 4
    offset = owner - me
    offset = jnp.where(offset > parts // 2, offset - parts, offset)
    offset = jnp.where(offset < -(parts // 2), offset + parts, offset)
    column = cell // height
    row = cell % height
    at = offset[:, None, :] * columns + column + HALO
    addr = jnp.where(
        (at >= 0) & (at < wide),
        ((row // LANES) * wide + at) * LANES + row % LANES,
        blocks * wide * LANES,
    )
    high_rows = rows_block + 2 * PAD
    at_row = row - (rows_block * me - PAD)
    whole_column = owner[:, None, :] * columns + column
    addr_rows = jnp.where(
        (at_row >= 0) & (at_row < high_rows) & (owner[:, None, :] < parts),
        ((whole_column // LANES) * high_rows + at_row) * LANES + whole_column % LANES,
        (length // LANES) * high_rows * LANES,
    )
    bound = jnp.arange(table, dtype=I32)
    start = jnp.sum((key[:, None, :] < bound[None, :, None]).astype(I32), axis=2)
    begin = start[:, 0 : 4 * parts : 4]
    mine = owner[:, None, :] == jnp.arange(parts, dtype=I32)[None, :, None]
    begin_own = jnp.sum(jnp.where(mine, begin[:, :, None], 0), axis=1)
    sender = jnp.arange(senders, dtype=I32)[:, None]
    slot = (
        jnp.minimum(owner, parts - 1) * (INFO * group * capacity)
        + (sender % group) * capacity
        + jnp.arange(hold, dtype=I32)[None, :]
        - begin_own
    )
    addr = addr.reshape(-1)
    weights = weights.reshape(-1)
    start = start.reshape(-1)

    acc = pltpu.VMEM((blocks * wide + 8, LANES), F32)
    static = dict(
        columns=columns,
        height=height,
        hold=hold,
        stencil=stencil,
        capacity=capacity,
        senders=senders,
        parts=parts,
        table=table,
    )
    per = group * stencil * hold
    meta = jnp.reshape(me, (1,)).astype(I32)
    smem_first = [
        pltpu.SMEM((per,), I32),
        pltpu.SMEM((per,), F32),
        pltpu.SMEM((group * hold,), F32),
        pltpu.SMEM((group * table,), I32),
        pltpu.SMEM((group * hold,), F32),
    ]
    work = [
        pltpu.VMEM((wide, height), BF),
        pltpu.VMEM((wide, height), BF),
    ] + [acc] * COPIES
    field0, reply, partial = pl.pallas_call(
        functools.partial(apply_kernel, first=True, **static),
        out_shape=[
            jax.ShapeDtypeStruct((columns, height), F32),
            jax.ShapeDtypeStruct((INFO, slots), F32),
            jax.ShapeDtypeStruct((8, LANES), F32),
        ],
        in_specs=[smem()] + [hbm()] * 5 + [vmem()] * 5,
        out_specs=[vmem()] * 3,
        scratch_shapes=smem_first
        + [acc, pltpu.VMEM((slots, LANES), F32), pltpu.VMEM((slots, LANES), F32)]
        + work
        + [pltpu.SemaphoreType.DMA((5,))],
        compiler_params=params(),
        name="apply_first",
    )(
        meta,
        addr,
        weights,
        source.reshape(-1),
        start,
        precision.reshape(-1),
        std,
        std_l,
        std_r,
        lat2,
        lon2,
    )

    def total_of(values):
        spread = jnp.broadcast_to(values[None], (parts * levels,) + values.shape)
        everyone = lax.all_to_all(
            spread, ("pencil", "lev"), split_axis=0, concat_axis=0, tiled=True
        )
        return jnp.sum(everyone, axis=0)

    replies = lax.all_to_all(
        jnp.broadcast_to(reply[None], (parts, INFO, slots)),
        "pencil",
        split_axis=0,
        concat_axis=0,
        tiled=True,
    )
    moments = total_of(partial)
    norm0, quad0 = moments[0, 0], moments[0, 1]
    back_all = replies[:, stencil + 2, :].reshape(-1)

    field1, second = pl.pallas_call(
        functools.partial(apply_kernel, first=False, **static),
        out_shape=[
            jax.ShapeDtypeStruct((columns, height), F32),
            jax.ShapeDtypeStruct((8, slots), F32),
        ],
        in_specs=[smem()] + [hbm()] * 4 + [vmem()] * 5,
        out_specs=[vmem()] * 2,
        scratch_shapes=[
            pltpu.SMEM((per,), I32),
            pltpu.SMEM((per,), F32),
            pltpu.SMEM((parts * slots,), F32),
            pltpu.SMEM((group * table,), I32),
            pltpu.VMEM((slots, LANES), F32),
        ]
        + work
        + [pltpu.SemaphoreType.DMA((5,))],
        compiler_params=params(),
        name="apply_second",
    )(meta, addr, weights, back_all, start, std, std_l, std_r, lat2, lon2)

    weight = reply[stencil]
    z0 = reply[stencil + 1]
    u = reply[stencil + 2]
    y0 = reply[stencil + 3]
    step0 = norm0 / (norm0 + quad0)
    resid = z0 - step0 * (z0 + u)
    image = y0 - step0 * (y0 + second[0])
    lanes = jnp.arange(LANES)[None, :]
    sums = [
        jnp.sum(resid * image),
        jnp.sum(resid * y0),
        jnp.sum(weight * image * image),
        jnp.sum(weight * image * y0),
    ]
    values = jnp.zeros((8, LANES), F32)
    for i, value in enumerate(sums):
        values = jnp.where(lanes == i, value, values)
    totals = total_of(values)
    norm1, cross, quad1, quad01 = (totals[0, i] for i in range(4))
    ratio = norm1 / norm0
    curvature = (
        norm1
        + 2.0 * ratio * cross
        + ratio * ratio * norm0
        + quad1
        + 2.0 * ratio * quad01
        + ratio * ratio * quad0
    )
    step1 = norm1 / curvature
    coef = jnp.stack([step0 + step1 * (1.0 - step0 + ratio), -step0 * step1])

    by_chunk = replies.reshape(parts, INFO, chunks, group * capacity)
    by_chunk = jnp.transpose(by_chunk, (2, 0, 1, 3)).reshape(-1)
    acc_rows = pltpu.VMEM(((length // LANES) * high_rows + 8, LANES), F32)
    control, increment = pl.pallas_call(
        functools.partial(
            final_kernel,
            hold=hold,
            stencil=stencil,
            capacity=capacity,
            senders=senders,
            parts=parts,
            length=length,
        ),
        out_shape=[
            jax.ShapeDtypeStruct((rows_block, length), F32),
            jax.ShapeDtypeStruct((columns, height), F32),
        ],
        in_specs=[smem()] + [hbm()] * 5 + [vmem()] * 5,
        out_specs=[vmem()] * 2,
        scratch_shapes=[
            pltpu.SMEM((per,), I32),
            pltpu.SMEM((group * hold,), I32),
            pltpu.SMEM((group * LANES,), I32),
            pltpu.SMEM((group * hold,), I32),
            pltpu.SMEM((parts * INFO * group * capacity,), F32),
            pltpu.VMEM((rows_block, length), BF),
            pltpu.VMEM((rows_block, length), BF),
        ]
        + [acc_rows] * COPIES
        + [pltpu.SemaphoreType.DMA((5,))],
        compiler_params=params(),
        name="outputs",
    )(
        coef,
        addr_rows.reshape(-1),
        listed.reshape(-1),
        amount.reshape(-1),
        slot.reshape(-1),
        by_chunk,
        std,
        field0,
        field1,
        lat1,
        lon1,
    )
    return control[None], increment[None]


def solution(mesh):
    return jax.shard_map(
        body,
        mesh=mesh,
        in_specs=(
            P("lev", "pencil", None),
            P("lev", None),
            P("lev", None),
            P(("pencil", "lev"), None),
            P(("pencil", "lev"), None),
            P(("pencil", "lev"), None),
            P(("pencil", "lev")),
            P(("pencil", "lev")),
            P(("pencil", "lev")),
        ),
        out_specs=(P("lev", "pencil", None), P("lev", "pencil", None)),
        check_vma=False,
    )
```

time: 2400 us -> 273 us (0.11)
  other arithmetic: 986 us -> 9.28 us
  blocking collectives: 678 us -> 0 us
  local copies, waits for them, and re-layouts: 494 us -> 16.4 us
  waiting for transfers between devices: 188 us -> 22.2 us
  Pallas kernels: 0 us -> 149 us
  starting transfers between devices: 27 us -> 64.4 us
    all_to_all x3 -> x0, blocking collectives: 521 us -> none  [the longest x2 424 us: adjoint(): lax.all_to_all(jnp.swapaxes(along_y, 1, 2), 'pencil', split_axis=1, conca...]
    gather x4 -> x0, local copies, waits for them, and re-layouts: 348 us -> none  [body(): smoothed.reshape(-1)[stencil]]
    add x6 -> x0, other arithmetic: 244 us -> none  [the longest x3 230 us: smooth(): result + kernel_taps[:, offset][:, None, None] * padded[:, :, offset:offs...]
    reduce_sum x6 -> x5, other arithmetic: 221 us -> 1.66 us  [the longest x1 0.8 us: body(): jnp.sum((key[:, None, :] < bound[None, :, None]).astype(I32), axis=2)]
    mul x12 -> x3, other arithmetic: 210 us -> 0.62 us  [the longest x1 0.59 us: body(): source = precision * recv[:, 2 * stencil, :]]
    all_to_all x4, waiting for transfers between devices: 188 us -> 21.8 us  [the longest x2 13.8 us: total_of(): lax.all_to_all(spread, ('pencil', 'lev'), split_axis=0, concat_axis=0, ti...]
    transpose x3 -> x0, other arithmetic: 160 us -> none  [adjoint(): jnp.swapaxes(along_y, 1, 2)]
    psum x3 -> x0, blocking collectives: 157 us -> none  [the longest x2 99.7 us: total_squares(): return lax.psum(jnp.sum(values * values), ('pencil', 'lev'))]
  transfers between devices with their start and end apart: 4 -> 6, of which waited for: 3 -> 4; matrix products, arithmetic and copies ran while one was open for 0% -> 4% of each run, Pallas kernels for 0% -> 3%
where the time goes in v1:
time: 273 us; the launch traced here: 271 us
  Pallas kernels  149 us (55%)
  starting transfers between devices  64.4 us (24%)
  waiting for transfers between devices  22.2 us (8%)
  local copies, waits for them, and re-layouts  16.4 us (6%)
  between operations  9.31 us (3%)
  other arithmetic  9.28 us (3%)
    pallas_call x1, Pallas kernels, body(): pl.pallas_call(functools.partial(apply_kernel, first=True, **static), out...  62 us
    all_to_all x2, starting transfers between devices, total_of(): lax.all_to_all(spread, ('pencil', 'lev'), split_axis=0, concat_axis=0, ti...  48.7 us
    pallas_call x1, Pallas kernels, body(): pl.pallas_call(functools.partial(apply_kernel, first=False, **static), ou...  43.2 us
    pallas_call x1, Pallas kernels, body(): pl.pallas_call(functools.partial(final_kernel, hold=hold, stencil=stencil...  33 us
    all_to_all x2, waiting for transfers between devices, total_of(): lax.all_to_all(spread, ('pencil', 'lev'), split_axis=0, concat_axis=0, ti...  13.8 us
    unnamed x24, local copies, waits for them, and re-layouts  8.3 us
    all_to_all x1, waiting for transfers between devices, body(): lax.all_to_all(jnp.broadcast_to(reply[None], (parts, INFO, slots)), 'penc...  8.01 us
    all_to_all x1, starting transfers between devices, body(): lax.all_to_all(packed, 'pencil', split_axis=0, concat_axis=0, tiled=True)  7.28 us
  transfers between devices with their start and end apart: 6, of which 4 were waited for; matrix products, arithmetic and copies ran while one was open for 4% of the time, Pallas kernels for 3%

profile of v1, /device:TPU:0, one launch (start us, length us, event | category | flops | bytes accessed | tf_op | source)
XLA Modules:
  0.0 271.1 jit_solution(15967349706161366138)
XLA Ops:
  1.3 1.5 copy.17.owner
  2.8 1.5 copy.18.cells
  4.2 1.5 copy.19.weights
  5.7 1.3 pad_maximum_fusion.extra
  7.0 4.2 %pack.1 = f32[8,40,256]{2,1,0:T(8,128)} custom-call(s32[1]{0:T(128)S(6)} %copy.40.counts, s32[256,1]{1,0:T(8,128)} %copy.17.owner, s32[256,16]{1,0:T(8,128)} %copy.18.cells, f32[256,16]{1,0:T(8,128)} %copy.19.weights, f32[2,256]{1,0:T(2,128)} %pad_maximum_fusion.extra), custom_call_target="tpu_custom_call" | custom-call | tf_op jit(solution)/shard_map/pack/pallas_call | solution.py:589
  11.1 7.3 %all-to-all-start = ((f32[8,40,256]{2,1,0:T(8,128)}), f32[8,40,256]{2,1,0:T(8,128)S(1)}, u32[]{:S(2)}, u32[]{:S(2)}) async-start(f32[8,40,256]{2,1,0:T(8,128)} %pack.1), calls=%async_computation | async-start | bytes 655360 | tf_op jit(solution)/shard_map/all_to_all | solution.py:605
  18.4 1.1 slice_bitcast_fusion
  19.5 4.8 %collective-permute-start.1 = (f32[32,2048]{1,0:T(8,128)S(1)}, f32[32,2048]{1,0:T(8,128)S(1)}, u32[]{:S(2)}, u32[]{:S(2)}) collective-permute-start(f32[32,2048]{1,0:T(8,128)S(1)} %get-tuple-element.34), channel_id=1, source_target_pairs={{0,28},{4,0},{8,4},{12,8},{16,12},{20,16},{24,20},{28,24},{1,29},{... | collective-permute-start | bytes 786440 | tf_op jit(solution)/shard_map/ppermute | solution.py:587
  24.3 7.1 %bands.1 = (bf16[2,3,512,256]{3,2,1,0:T(8,128)(2,1)}, bf16[2,256,320]{2,1,0:T(8,128)(2,1)}, bf16[2,256,288]{2,1,0:T(8,128)(2,1)}, bf16[2,512,256]{2,1,0:T(8,128)(2,1)}) custom-call(f32[31]{0:T(128)} %bitcast.99, f32[31]{0:T(128)} %bitcast.100), custom_call_target="tpu_custom_call" | custom-call | tf_op jit(solution)/shard_map/bands/pallas_call | solution.py:608
  32.2 0.7 copy.26
  33.5 0.7 copy.25
  34.8 0.8 convert_reduce_fusion
  36.0 0.7 copy-done
  36.8 62.0 %apply_first.1 = (f32[512,2048]{1,0:T(8,128)}, f32[24,512]{1,0:T(8,128)}, f32[8,128]{1,0:T(8,128)}) custom-call(s32[1]{0:T(128)} %bitcast.refs_0_, s32[32768]{0:T(1024)} %bitcast.68, f32[32768]{0:T(1024)} %bitcast.66, f32[2048]{0:T(1024)} %mul.96.refs_3_, s32[1024]{0:T(1024)} %bitcast.77, f32[2048]{0:T(1024)} %bitcast.75, f32[512,2048]{1,0:T(8,128)} %bitcast.61, ...), custom_call_target="tpu_custom_call" | custom-call | tf_op jit(solution)/shard_map/apply_first/pallas_call | solution.py:689
  98.8 1.3 broadcast_in_dim.100
  100.1 34.4 %all-to-all-start.1 = ((f32[32,8,128]{2,1,0:T(8,128)}), f32[32,8,128]{2,1,0:T(8,128)S(1)}, u32[]{:S(2)}, u32[]{:S(2)}) async-start(f32[32,8,128]{2,1,0:T(8,128)} %broadcast_in_dim.100), calls=%async_computation.1 | async-start | bytes 262144 | tf_op jit(solution)/shard_map/all_to_all | solution.py:720
  134.6 8.1 %all-to-all-done.1 = f32[32,8,128]{2,1,0:T(8,128)S(1)} async-done(((f32[32,8,128]{2,1,0:T(8,128)}), f32[32,8,128]{2,1,0:T(8,128)S(1)}, u32[]{:S(2)}, u32[]{:S(2)}) %all-to-all-start.1) | async-done | bytes 131104 | tf_op jit(solution)/shard_map/all_to_all | solution.py:720
  142.7 1.6 broadcast_in_dim.102
  144.3 3.7 %all-to-all-start.2 = ((f32[8,24,512]{2,1,0:T(8,128)}), f32[8,24,512]{2,1,0:T(8,128)S(1)}, u32[]{:S(2)}, u32[]{:S(2)}) async-start(f32[8,24,512]{2,1,0:T(8,128)} %broadcast_in_dim.102), calls=%async_computation.2 | async-start | bytes 786432 | tf_op jit(solution)/shard_map/all_to_all | solution.py:725
  148.2 0.9 fusion.30
  152.0 8.0 %all-to-all-done.2 = f32[8,24,512]{2,1,0:T(8,128)S(1)} async-done(((f32[8,24,512]{2,1,0:T(8,128)}), f32[8,24,512]{2,1,0:T(8,128)S(1)}, u32[]{:S(2)}, u32[]{:S(2)}) %all-to-all-start.2) | async-done | bytes 393248 | tf_op jit(solution)/shard_map/all_to_all | solution.py:725
  160.7 43.2 %apply_second.1 = (f32[512,2048]{1,0:T(8,128)}, f32[8,512]{1,0:T(8,128)}) custom-call(s32[1]{0:T(128)} %bitcast.refs_0_, s32[32768]{0:T(1024)} %bitcast.69, f32[32768]{0:T(1024)} %bitcast.67, f32[4096]{0:T(1024)} %bitcast.79, s32[1024]{0:T(1024)} %bitcast.78, f32[512,2048]{1,0:T(8,128)} %bitcast.62, f32[32,2048]{1,0:T(8,128)} %copy-done.1, ...), custom_call_target="tpu_custom_call" | custom-call | tf_op jit(solution)/shard_map/apply_second/pallas_call | solution.py:736
  203.8 0.7 slice.86
  204.6 0.7 multiply_reduce_fusion.1
  205.3 0.6 compare_select_fusion.5
  205.9 2.0 select_select_fusion
  207.9 0.7 broadcast_in_dim.111
  208.6 14.3 %all-to-all-start.3 = ((f32[32,8,128]{2,1,0:T(8,128)}), f32[32,8,128]{2,1,0:T(8,128)S(1)}, u32[]{:S(2)}, u32[]{:S(2)}) async-start(f32[32,8,128]{2,1,0:T(8,128)} %broadcast_in_dim.111), calls=%async_computation.3 | async-start | bytes 262144 | tf_op jit(solution)/shard_map/all_to_all | solution.py:720
  223.0 0.7 copy.27
  224.3 0.9 copy.31
  225.2 5.7 %all-to-all-done.3 = f32[32,8,128]{2,1,0:T(8,128)S(1)} async-done(((f32[32,8,128]{2,1,0:T(8,128)}), f32[32,8,128]{2,1,0:T(8,128)S(1)}, u32[]{:S(2)}, u32[]{:S(2)}) %all-to-all-start.3) | async-done | bytes 131104 | tf_op jit(solution)/shard_map/all_to_all | solution.py:720
  237.9 33.0 %outputs.1 = (f32[256,4096]{1,0:T(8,128)}, f32[512,2048]{1,0:T(8,128)}) custom-call(f32[2]{0:T(128)} %pad_maximum_fusion.1.coef, s32[32768]{0:T(1024)} %bitcast.70, s32[2048]{0:T(1024)} %bitcast.80, s32[1024]{0:T(1024)} %bitcast.88, s32[2048]{0:T(1024)} %fusion.25.slot_h, f32[98304]{0:T(1024)} %bitcast.65, f32[512,2048]{1,0:T(8,128)} %bitcast.63, ...), custom_call_target="tpu_custom_call" | custom-call | tf_op jit(solution)/shard_map/outputs/pallas_call | solution.py:791
  (40 shorter events, 6.4 us)
Async XLA Ops:
  11.1 20.3 %all-to-all-start = ((f32[8,40,256]{2,1,0:T(8,128)}), f32[8,40,256]{2,1,0:T(8,128)S(1)}, u32[]{:S(2)}, u32[]{:S(2)}) async-start(f32[8,40,256]{2,1,0:T(8,128)} %pack.1), calls=%async_computation | async-start | bytes 655360 | tf_op jit(solution)/shard_map/all_to_all | solution.py:605
  19.5 16.5 %collective-permute-start.1 = (f32[32,2048]{1,0:T(8,128)S(1)}, f32[32,2048]{1,0:T(8,128)S(1)}, u32[]{:S(2)}, u32[]{:S(2)}) collective-permute-start(f32[32,2048]{1,0:T(8,128)S(1)} %get-tuple-element.34), channel_id=1, source_target_pairs={{0,28},{4,0},{8,4},{12,8},{16,12},{20,16},{24,20},{28,24},{1,29},{... | collective-permute-start | bytes 786440 | tf_op jit(solution)/shard_map/ppermute | solution.py:587
  24.3 11.7 %collective-permute-start = (f32[32,2048]{1,0:T(8,128)S(1)}, f32[32,2048]{1,0:T(8,128)S(1)}, u32[]{:S(2)}, u32[]{:S(2)}) collective-permute-start(f32[32,2048]{1,0:T(8,128)S(1)} %get-tuple-element.35), channel_id=1, source_target_pairs={{0,4},{4,8},{8,12},{12,16},{16,20},{20,24},{24,28},{28,0},{1,5},{5... | collective-permute-start | bytes 786440 | tf_op jit(solution)/shard_map/ppermute | solution.py:586
  32.2 3.9 %copy-start.2 = (f32[8,1,256]{2,1,0:T(1,128)}, f32[8,1,256]{2,1,0:T(1,128)S(1)}, u32[]{:S(2)}) copy-start(f32[8,1,256]{2,1,0:T(1,128)S(1)} %get-tuple-element.38) | copy-start | bytes 24580
  36.0 0.7 copy-start
  36.0 0.8 copy-start.1
  36.8 111.3 %copy-start.3 = (s32[8,128]{1,0:T(8,128)S(1)}, s32[8,128]{1,0:T(8,128)}, u32[]{:S(2)}) copy-start(s32[8,128]{1,0:T(8,128)} %convert_reduce_fusion) | copy-start | bytes 12292
  100.1 42.6 %all-to-all-start.1 = ((f32[32,8,128]{2,1,0:T(8,128)}), f32[32,8,128]{2,1,0:T(8,128)S(1)}, u32[]{:S(2)}, u32[]{:S(2)}) async-start(f32[32,8,128]{2,1,0:T(8,128)} %broadcast_in_dim.100), calls=%async_computation.1 | async-start | bytes 262144 | tf_op jit(solution)/shard_map/all_to_all | solution.py:720
  144.3 15.7 %all-to-all-start.2 = ((f32[8,24,512]{2,1,0:T(8,128)}), f32[8,24,512]{2,1,0:T(8,128)S(1)}, u32[]{:S(2)}, u32[]{:S(2)}) async-start(f32[8,24,512]{2,1,0:T(8,128)} %broadcast_in_dim.102), calls=%async_computation.2 | async-start | bytes 786432 | tf_op jit(solution)/shard_map/all_to_all | solution.py:725
  208.6 22.3 %all-to-all-start.3 = ((f32[32,8,128]{2,1,0:T(8,128)}), f32[32,8,128]{2,1,0:T(8,128)S(1)}, u32[]{:S(2)}, u32[]{:S(2)}) async-start(f32[32,8,128]{2,1,0:T(8,128)} %broadcast_in_dim.111), calls=%async_computation.3 | async-start | bytes 262144 | tf_op jit(solution)/shard_map/all_to_all | solution.py:720

commit v2 on v1

v2 whole, which is shorter than its diff:
```python
import functools

import jax
import jax.numpy as jnp
import numpy as np
from jax import lax
from jax.experimental import pallas as pl
from jax.experimental.pallas import tpu as pltpu
from jax.sharding import PartitionSpec as P


BF = jnp.bfloat16
F32 = jnp.float32
I32 = jnp.int32
LANES = 128
WIDE = 256
HALO = 32
PAD = 16
PACK = 40
GROUP = 8
COPIES = 4
VMEM_LIMIT = 58 * 1024 * 1024


def vmem():
    return pl.BlockSpec(memory_space=pltpu.VMEM)


def smem():
    return pl.BlockSpec(memory_space=pltpu.SMEM)


def hbm():
    return pl.BlockSpec(memory_space=pl.ANY)


def params():
    return pltpu.CompilerParams(vmem_limit_bytes=VMEM_LIMIT)


def split2(x):
    high = x.astype(BF)
    return high, (x - high.astype(F32)).astype(BF)


def split3(x):
    high = x.astype(BF)
    rest = x - high.astype(F32)
    mid = rest.astype(BF)
    return high, mid, (rest - mid.astype(F32)).astype(BF)


def mm(a, b):
    return jnp.dot(a, b, preferred_element_type=F32)


def mm_parts(a_parts, b_parts):
    (ah, al), (bh, bl) = a_parts, b_parts
    return mm(ah, bh) + (mm(al, bh) + mm(ah, bl))


def iota(shape, dim):
    return lax.broadcasted_iota(I32, shape, dim)


def pack_kernel(
    counts, owner, cells, weights, depart, prec, out, *, parts, columns, height, margin
):
    stencil, hold = cells.shape
    shift = height.bit_length() - 1
    block = height // parts
    reach = 2 * margin
    row_id = iota((hold, hold), 0)
    col_id = iota((hold, hold), 1)
    eye = row_id == col_id
    col_f = col_id.astype(F32)
    live = iota((1, hold), 1) < counts[0]
    cell = cells[...]
    column = lax.shift_right_logical(cell, jnp.full(cell.shape, shift, I32))
    row = cell & (height - 1)

    def any_of(mask):
        return jnp.max(jnp.where(mask, 1.0, 0.0), axis=0, keepdims=True)

    def turn(line):
        return jnp.sum(jnp.where(eye, line, 0.0), axis=1, keepdims=True)

    left = any_of(column < reach)
    right = any_of(column >= columns - reach)
    side = left + 3.0 * right - 2.0 * left * right
    base = jnp.where(live, owner[...].astype(F32) * 4.0, 4.0 * parts)
    key = jnp.where(live, base + side, base)
    key_col = turn(key)
    before = (key_col < key) | ((key_col == key) & (row_id < col_id))
    rank = jnp.sum(jnp.where(before, 1.0, 0.0), axis=0, keepdims=True)
    begin = jnp.sum(jnp.where(key_col < base, 1.0, 0.0), axis=0, keepdims=True)
    rank_col = turn(rank)
    perm = jnp.where(rank_col == col_f, 1.0, 0.0).astype(BF)

    def sort(values):
        total = None
        for part in split3(values):
            term = mm(part, perm)
            total = term if total is None else total + term
        return total

    weight = jnp.where(live, prec[...], 0.0)
    rest = [weight * depart[...], weight, key, rank - begin, jnp.zeros((4, hold), F32)]
    values = [cell.astype(F32), weights[...]] + rest
    ordered = sort(jnp.concatenate(values, axis=0))
    line = iota((8, hold), 0)
    tail = ordered[2 * stencil : 2 * stencil + 8, :]
    for i in range(3):
        if i * hold <= 4 * parts:
            begins = jnp.sum(
                jnp.where(key_col < (col_f + float(i * hold)), 1.0, 0.0), axis=0, keepdims=True
            )
            tail = jnp.where(line == 5 + i, begins, tail)
    last = (line == 7) & (iota((8, hold), 1) == hold - 1)

    def per_part(part, carry):
        low = part * block - margin
        high = (part + 1) * block + margin
        flag = jnp.where(live, any_of((row >= low) & (row < high)), 0.0)
        place = jnp.sum(jnp.where(col_id < row_id, flag, 0.0), axis=1, keepdims=True)
        chosen = (place == col_f) & (turn(flag) > 0.0)
        listed = jnp.sum(jnp.where(chosen, rank_col, 0.0), axis=0, keepdims=True)
        amount = jnp.sum(flag, axis=1, keepdims=True)
        out[part, 0 : 2 * stencil, :] = ordered[0 : 2 * stencil, :]
        out[part, 2 * stencil : 2 * stencil + 8, :] = jnp.where(
            line == 4, listed, jnp.where(last, amount, tail)
        )
        return carry

    lax.fori_loop(0, parts, per_part, 0)


class Layout:
    def __init__(self, senders, hold, stencil, parts):
        lines = hold // LANES
        self.table = 3 * hold
        sizes = dict(
            addr=stencil * lines, rows=stencil * lines, listed=lines, slot=lines, back=lines
        )
        sizes.update(start=3 * lines)
        self.ints = {}
        at = 0
        for name, size in sizes.items():
            self.ints[name] = (at, size)
            at += senders * size
        self.int_rows = at
        self.floats = {}
        at = 0
        for name, size in dict(wgt=stencil * lines, val=lines, prec=lines).items():
            self.floats[name] = (at, size)
            at += senders * size
        self.float_rows = at


def unpack_kernel(
    meta, recv, ints, floats, *, layout, parts, columns, height, capacity, stencil, group
):
    senders, _, hold = recv.shape
    lines = hold // LANES
    me = meta[0]
    shift = height.bit_length() - 1
    wide = columns + 2 * HALO
    block = height // parts
    high_rows = block + 2 * PAD
    length = columns * parts
    slots = senders * capacity

    def put(ref, place, sender, value):
        begin, size = place
        count = value.shape[0]
        for i in range(lines):
            part = value[:, i * LANES : (i + 1) * LANES]
            if count % 8 == 0:
                at = pl.multiple_of(begin + sender * size + i * count, 8)
                ref[pl.ds(at, count), :] = part
            else:
                for j in range(count):
                    ref[pl.ds(begin + sender * size + i + j * lines, 1), :] = part[j : j + 1]

    def right(x, by):
        return lax.shift_right_logical(x, jnp.full(x.shape, by, I32))

    def per_sender(sender, carry):
        cell = recv[sender, 0:stencil, :].astype(I32)
        tail = recv[sender, 2 * stencil : 2 * stencil + 8, :]
        whole = tail.astype(I32)
        key = whole[2:3, :]
        pos = whole[3:4, :]
        owner = right(key, 2)
        offset = owner - me
        offset = jnp.where(offset > parts // 2, offset - parts, offset)
        offset = jnp.where(offset < -(parts // 2), offset + parts, offset)
        column = right(cell, shift)
        row = cell & (height - 1)
        at = offset * columns + column + HALO
        addr = jnp.where(
            (at >= 0) & (at < wide),
            (right(row, 7) * wide + at) * LANES + (row & (LANES - 1)),
            (height // LANES) * wide * LANES,
        )
        at_row = row - (block * me - PAD)
        across = owner * columns + column
        rows = jnp.where(
            (at_row >= 0) & (at_row < high_rows) & (owner < parts),
            (right(across, 7) * high_rows + at_row) * LANES + (across & (LANES - 1)),
            (length // LANES) * high_rows * LANES,
        )
        within = lax.rem(sender, group) * capacity + pos
        owner = jnp.minimum(owner, parts - 1)
        put(ints, layout.ints["addr"], sender, addr)
        put(ints, layout.ints["rows"], sender, rows)
        put(ints, layout.ints["listed"], sender, whole[4:5, :])
        put(ints, layout.ints["slot"], sender, owner * (stencil * group * capacity) + within)
        put(ints, layout.ints["back"], sender, owner * slots + sender * capacity + pos)
        put(ints, layout.ints["start"], sender, whole[5:8, :])
        put(floats, layout.floats["wgt"], sender, recv[sender, stencil : 2 * stencil, :])
        put(floats, layout.floats["val"], sender, tail[0:1, :])
        put(floats, layout.floats["prec"], sender, tail[1:2, :])
        return carry

    lax.fori_loop(0, senders, per_sender, 0)


def band(shape, taps, shift):
    distance = iota(shape, 1) - iota(shape, 0) + shift
    result = jnp.zeros(shape, F32)
    for tap in range(taps.shape[0]):
        result = jnp.where(distance == tap, taps[tap], result)
    return result


def band_rev(shape, taps, shift):
    distance = iota(shape, 0) - iota(shape, 1) + shift
    result = jnp.zeros(shape, F32)
    for tap in range(taps.shape[0]):
        result = jnp.where(distance == tap, taps[tap], result)
    return result


def exact_nt(a, b):
    return lax.dot_general(
        a,
        b,
        (((1,), (1,)), ((), ())),
        precision=lax.Precision.HIGHEST,
        preferred_element_type=F32,
    )


def store_split(ref, index, value):
    high, low = split2(value)
    ref[(0,) + index] = high
    ref[(1,) + index] = low


def bands_kernel(kx, ky, lat2, lon2, lat1, lon1, *, rows_block):
    margin = kx.shape[0] // 2
    window = lat2.shape[2]
    first = band((window, window), ky, margin)
    reach = first[LANES : LANES + WIDE, :]
    place = iota((window, window), 1)
    for variant in range(3):
        kept = first
        if variant == 0:
            kept = jnp.where(place >= LANES, first, 0.0)
        if variant == 2:
            kept = jnp.where(place < LANES + WIDE, first, 0.0)
        store_split(lat2, (variant,), exact_nt(kept, reach))
    size = lon2.shape[1]
    wide = size + 2 * HALO
    depth = (wide + 32 + LANES - 1) // LANES * LANES
    second = band((wide, depth), kx, -(16 - margin))
    store_split(lon2, (), exact_nt(second[HALO : HALO + size, :], second))
    store_split(lat1, (), band_rev((rows_block, rows_block + 2 * PAD), ky, PAD + margin))
    store_split(lon1, (), band((2 * WIDE, WIDE), kx, LANES + margin))


def pairs(low, high, action):
    def step(i, carry):
        one = low + 2 * i
        action(one, jnp.minimum(one + 1, high - 1), one + 1 < high)
        return carry

    lax.fori_loop(0, lax.shift_right_logical(high - low + 1, 1), step, 0)


def zero_all(refs):
    rows = refs[0].shape[0]
    step = 256

    def clear(i, carry):
        for ref in refs:
            ref[pl.ds(pl.multiple_of(i * step, 8), step), :] = jnp.zeros((step, LANES), F32)
        return carry

    whole = rows // step
    lax.fori_loop(0, whole, clear, 0)
    if rows % step:
        for ref in refs:
            ref[whole * step : rows, :] = jnp.zeros((rows % step, LANES), F32)


def scatter_entries(copies, entries, lane):
    for start in range(0, len(entries), len(copies)):
        group = []
        for ref, (address, value) in zip(copies, entries[start : start + len(copies)]):
            line = lax.shift_right_logical(address, 7)
            spread = jnp.where(lane == (address & (LANES - 1)), value, 0.0)
            group.append((ref, line, ref[pl.ds(line, 1), :] + spread))
        for ref, line, value in group:
            ref[pl.ds(line, 1), :] = value


def spot(sender, idx, per, stencil):
    return sender * per + idx + lax.shift_right_logical(idx, 7) * ((stencil - 1) * LANES)


def copy_parts(layout, source, target, place, chunk, chunks, group, sem):
    begin, size = place
    words = group * size * LANES
    at = begin * LANES + chunk * words
    return pltpu.make_async_copy(source.at[pl.ds(at, words)], target, sem)


def apply_kernel(
    *refs, first, layout, columns, height, hold, stencil, capacity, senders, parts, levels
):
    refs = list(refs)

    def take(count):
        taken = refs[:count]
        del refs[:count]
        return taken

    meta, ints, floats = take(3)
    if not first:
        back, moments, column_info = take(3)
    std_h, std_l_h, std_r_h, lat2_h, lon2_h = take(5)
    field_h, send = take(2)
    if first:
        factors_out, info_out = take(2)
    addr, wgt, start = take(3)
    if first:
        val, prec, std_flat, info, picked = take(5)
    sums, high_s, low_s, std, std_l, std_r, lat2, lon2, field = take(9)
    copies = take(COPIES)
    sems, in_sems, out_sems = take(3)

    me = meta[0]
    wide = columns + 2 * HALO
    blocks = height // LANES
    group = min(GROUP, senders)
    chunks = senders // group
    slots = senders * capacity
    lane = iota((1, LANES), 1)
    per = stencil * hold
    table = layout.table

    def chunk_copies(chunk):
        todo = [
            (ints, addr, layout.ints["addr"]),
            (floats, wgt, layout.floats["wgt"]),
            (ints, start, layout.ints["start"]),
        ]
        if first:
            todo.append((floats, val, layout.floats["val"]))
            todo.append((floats, prec, layout.floats["prec"]))
        return [
            copy_parts(layout, source, target, place, chunk, chunks, group, sems.at[i])
            for i, (source, target, place) in enumerate(todo)
        ]

    def load_chunk(chunk):
        for copy in chunk_copies(chunk):
            copy.start()
        for copy in chunk_copies(chunk):
            copy.wait()

    pending = []
    if chunks == 1:
        pending = chunk_copies(0)
        for copy in pending:
            copy.start()
    operands = [
        pltpu.make_async_copy(source, target, in_sems.at[i])
        for i, (source, target) in enumerate(
            (
                (std_h, std),
                (std_l_h, std_l),
                (std_r_h, std_r),
                (lat2_h, lat2),
                (lon2_h, lon2),
            )
        )
    ]
    for copy in operands:
        copy.start()
    zero_all(copies)
    zero_all([sums] + ([info] if first else []))
    for copy in pending:
        copy.wait()

    after = lax.rem(me + 1, parts)
    ahead = lax.rem(me + parts - 1, parts)

    def start_of(sender, key):
        return start[sender * table + key]

    def entries_of(sender, idx, value):
        base = spot(sender, idx, per, stencil)
        return [
            (addr[base + k * LANES], wgt[base + k * LANES] * value) for k in range(stencil)
        ]

    def scatter_chunk(chunk):
        def per_sender(sender, carry):
            for owner, low, high in ((me, 0, 4), (after, 1, 3), (ahead, 2, 4)):
                begin = start_of(sender, owner * 4)

                def value_of(idx, owner=owner, begin=begin):
                    if first:
                        return val[sender * hold + idx]
                    place = (chunk * group + sender) * capacity + idx - begin
                    return back[owner * (8 * LANES) + place]

                def action(one, two, has_two, value_of=value_of):
                    second = jnp.where(has_two, value_of(two), 0.0)
                    scatter_entries(
                        copies,
                        entries_of(sender, one, value_of(one)) + entries_of(sender, two, second),
                        lane,
                    )

                pairs(
                    start_of(sender, owner * 4 + low), start_of(sender, owner * 4 + high), action
                )
            return carry

        lax.fori_loop(0, group, per_sender, 0)

    def over_chunks(work):
        if chunks == 1:
            work(0)
        else:

            def step(chunk, carry):
                load_chunk(chunk)
                work(chunk)
                return carry

            lax.fori_loop(0, chunks, step, 0)

    over_chunks(scatter_chunk)
    for copy in operands:
        copy.wait()

    for jb in range(blocks):
        lanes = slice(jb * LANES, (jb + 1) * LANES)
        for low, size, source in (
            (0, HALO, std_l),
            (HALO, columns, std),
            (HALO + columns, HALO, std_r),
        ):
            rows = slice(jb * wide + low, jb * wide + low + size)
            total = copies[0][rows, :]
            for ref in copies[1:]:
                total = total + ref[rows, :]
            high, lo = split2(total * source[:, lanes])
            high_s[low : low + size, lanes] = high
            low_s[low : low + size, lanes] = lo
        if first:
            std_flat[jb * wide + HALO : jb * wide + HALO + columns, :] = std[:, lanes]

    smoothed = copies[0]
    size = lon2.shape[1]
    count = height // WIDE
    outgoing = []
    for block in range(count):
        variant = 0 if block == 0 else (2 if block == count - 1 else 1)
        low = max(block * WIDE - LANES, 0)
        high = min(block * WIDE + WIDE + LANES, height)
        inner = slice(low - (block * WIDE - LANES), high - (block * WIDE - LANES))
        matrix = (lat2[0, variant, inner, :], lat2[1, variant, inner, :])
        along = mm_parts((high_s[:, low:high], low_s[:, low:high]), matrix)
        parts_y = split2(along)
        lanes = slice(block * WIDE, (block + 1) * WIDE)
        for part in range(columns // size):
            rows = slice(part * size, (part + 1) * size)
            window = slice(part * size, part * size + size + 2 * HALO)
            result = mm_parts(
                (lon2[0], lon2[1]), (parts_y[0][window, :], parts_y[1][window, :])
            )
            field[rows, lanes] = result
            scaled = result * std[rows, lanes]
            for half in range(WIDE // LANES):
                top = (block * (WIDE // LANES) + half) * wide + HALO + part * size
                smoothed[top : top + size, :] = scaled[:, half * LANES : (half + 1) * LANES]
        outgoing.append(
            pltpu.make_async_copy(field.at[:, lanes], field_h.at[:, lanes], out_sems.at[block])
        )
        outgoing[-1].start()

    def gather_chunk(chunk):
        def per_sender(sender, carry):
            begin = start_of(sender, me * 4)

            def gather(idx):
                slot = (chunk * group + sender) * capacity + idx - begin
                base = spot(sender, idx, per, stencil)
                total = [jnp.zeros((1, LANES), F32)] * 4
                for k in range(stencil):
                    address = addr[base + k * LANES]
                    line = lax.shift_right_logical(address, 7)
                    spread = jnp.where(
                        lane == (address & (LANES - 1)), wgt[base + k * LANES], 0.0
                    )
                    total[k % 4] = total[k % 4] + spread * smoothed[pl.ds(line, 1), :]
                    if first:
                        picked[pl.ds(k * slots + slot, 1), :] = (
                            spread * std_flat[pl.ds(line, 1), :]
                        )
                sums[pl.ds(slot, 1), :] = (total[0] + total[1]) + (total[2] + total[3])
                if first:
                    info[pl.ds(slot, 1), :] = jnp.where(
                        lane == 0,
                        prec[sender * hold + idx],
                        jnp.where(lane == 1, val[sender * hold + idx], 0.0),
                    )

            def action(one, two, has_two):
                gather(one)
                gather(two)

            pairs(begin, start_of(sender, me * 4 + 4), action)
            return carry

        lax.fori_loop(0, group, per_sender, 0)

    over_chunks(gather_chunk)

    def whole(x):
        return jnp.sum(x, axis=0, keepdims=True)

    total = jnp.sum(sums[...], axis=1, keepdims=True)
    lanes = iota((slots, LANES), 1)
    lines = slots // LANES
    if first:
        known = info[...]
        weight = known[:, 0:1]
        source = known[:, 1:2]
        reply = weight * total
        known = jnp.where(lanes == 2, reply, jnp.where(lanes == 3, total, known))
        info_out[...] = known
        turned = known.T
        message = [turned[2:3, i * LANES : (i + 1) * LANES] for i in range(lines)]
        message.append(
            jnp.where(lane == 0, whole(source * total), jnp.where(lane == 1, whole(reply * total), 0.0))
        )
        message.append(jnp.zeros((8 - len(message), LANES), F32))
        message = jnp.concatenate(message, axis=0)
        ones = jnp.ones((8, LANES), BF)
        for k in range(stencil):
            row = None
            for part in split3(picked[k * slots : (k + 1) * slots, :]):
                term = lax.dot_general(
                    ones, part, (((1,), (1,)), ((), ())), preferred_element_type=F32
                )
                row = term if row is None else row + term
            factors_out[k : k + 1, :] = row[0:1, :]
    else:
        known = column_info[...]
        weight, source, reply, image0 = (known[:, i : i + 1] for i in range(4))
        slab = jnp.sum(moments[...], axis=0)[lines : lines + 1, :]
        length = slab[:, 0:1] / (slab[:, 0:1] + slab[:, 1:2])
        both = source + reply
        s_both = image0 + total
        resid = source - length * both
        s_resid = image0 - length * s_both
        values = [
            resid * s_resid,
            resid * s_both,
            both * s_both,
            resid * image0,
            both * image0,
            weight * s_resid * s_resid,
            weight * s_resid * s_both,
            weight * s_both * s_both,
            weight * s_resid * image0,
            weight * s_both * image0,
            source * image0,
            reply * image0,
        ]
        message = jnp.where(lane == len(values), length, 0.0)
        for i, value in enumerate(values):
            message = jnp.where(lane == i, whole(value), message)
        message = jnp.concatenate([message, jnp.zeros((7, LANES), F32)], axis=0)

    def send_to(i, carry):
        send[i] = message
        return carry

    lax.fori_loop(0, send.shape[0], send_to, 0)
    for copy in outgoing:
        copy.wait()


def final_kernel(
    ints,
    floats,
    factors_h,
    back,
    totals,
    std_h,
    field0_h,
    field1_h,
    lat1,
    lon1,
    control_h,
    increment_h,
    addr,
    listed,
    start,
    slot,
    back_at,
    val,
    factors,
    std,
    field0,
    field1,
    control,
    high_s,
    low_s,
    *rest,
    layout,
    hold,
    stencil,
    capacity,
    senders,
    parts,
    length,
):
    copies = rest[:COPIES]
    sems, in_sems, out_sems = rest[COPIES:]
    group = min(GROUP, senders)
    chunks = senders // group
    per = stencil * hold
    rows_block = control.shape[0]
    high_rows = rows_block + 2 * PAD
    lane = iota((1, LANES), 1)
    stride = group * capacity
    slots = senders * capacity

    def chunk_copies(chunk):
        todo = [
            (ints, addr, layout.ints["rows"]),
            (ints, listed, layout.ints["listed"]),
            (ints, start, layout.ints["start"]),
            (ints, slot, layout.ints["slot"]),
            (ints, back_at, layout.ints["back"]),
            (floats, val, layout.floats["val"]),
        ]
        result = [
            copy_parts(layout, source, target, place, chunk, chunks, group, sems.at[i])
            for i, (source, target, place) in enumerate(todo)
        ]
        words = parts * stencil * stride
        result.append(
            pltpu.make_async_copy(
                factors_h.at[pl.ds(chunk * words, words)], factors, sems.at[len(todo)]
            )
        )
        return result

    pending = []
    if chunks == 1:
        pending = chunk_copies(0)
        for copy in pending:
            copy.start()
    operands = [
        pltpu.make_async_copy(source, target, in_sems.at[i])
        for i, (source, target) in enumerate(
            ((std_h, std), (field0_h, field0), (field1_h, field1))
        )
    ]
    for copy in operands:
        copy.start()

    slabs = totals.shape[1]
    every = jnp.sum(totals[...], axis=0)
    norm0 = quad0 = None
    for i in range(slabs):
        line = every[i, 0:1, :]
        a, b = line[:, 10:11], line[:, 11:12]
        norm0 = a if norm0 is None else norm0 + a
        quad0 = b if quad0 is None else quad0 + b
    step0 = norm0 / (norm0 + quad0)
    norm1 = cross = quad1 = quad01 = jnp.zeros((1, 1), F32)
    for i in range(slabs):
        line = every[i, 0:1, :]
        v = [line[:, j : j + 1] for j in range(10)]
        shift = totals[0, i, 0:1, 12:13] - step0
        norm1 = norm1 + (v[0] + shift * (2.0 * v[1] + shift * v[2]))
        cross = cross + (v[3] + shift * v[4])
        quad1 = quad1 + (v[5] + shift * (2.0 * v[6] + shift * v[7]))
        quad01 = quad01 + (v[8] + shift * v[9])
    ratio = norm1 / norm0
    curvature = norm1 + quad1 + ratio * (
        2.0 * (cross + quad01) + ratio * (norm0 + quad0)
    )
    step1 = norm1 / curvature
    first = step0 + step1 * (1.0 - step0 + ratio)
    second = -step0 * step1
    first_line = jnp.broadcast_to(first, (1, LANES))
    second_line = jnp.broadcast_to(second, (1, LANES))

    zero_all(copies)
    for copy in operands:
        copy.wait()
    increment = field0
    increment[...] = std[...] * (first * field0[...] + second * field1[...])
    outgoing = [pltpu.make_async_copy(increment, increment_h, out_sems.at[0])]
    outgoing[0].start()

    def scatter_chunk():
        def per_sender(sender, carry):
            def entries_of(at, scale):
                idx = listed[sender * hold + at]
                place = slot[sender * hold + idx]
                base = spot(sender, idx, per, stencil)
                z0 = val[sender * hold + idx] * scale
                u = back[_back_index(back_at[sender * hold + idx], slots)] * scale
                value = first_line * z0 + second_line * u
                return [
                    (addr[base + k * LANES], factors[place + k * stride] * value)
                    for k in range(stencil)
                ]

            def action(one, two, has_two):
                scale = jnp.where(has_two, 1.0, 0.0)
                scatter_entries(copies, entries_of(one, 1.0) + entries_of(two, scale), lane)

            pairs(0, start[sender * layout.table + layout.table - 1], action)
            return carry

        lax.fori_loop(0, group, per_sender, 0)

    if chunks == 1:
        for copy in pending:
            copy.wait()
        scatter_chunk()
    else:

        def step(chunk, carry):
            for copy in chunk_copies(chunk):
                copy.start()
            for copy in chunk_copies(chunk):
                copy.wait()
            scatter_chunk()
            return carry

        lax.fori_loop(0, chunks, step, 0)

    pair = WIDE // LANES
    count = length // WIDE
    for block in range(count):
        pieces = []
        for half in range(pair):
            rows = slice((block * pair + half) * high_rows, (block * pair + half + 1) * high_rows)
            total = copies[0][rows, :]
            for ref in copies[1:]:
                total = total + ref[rows, :]
            pieces.append(total)
        along = mm_parts((lat1[0], lat1[1]), split2(jnp.concatenate(pieces, axis=1)))
        high, low = split2(along)
        high_s[:, block * WIDE : (block + 1) * WIDE] = high
        low_s[:, block * WIDE : (block + 1) * WIDE] = low

    def window(ref, block):
        low, high = block * WIDE - LANES, (block + 1) * WIDE + LANES
        if low < 0:
            return jnp.concatenate([ref[:, length + low : length], ref[:, 0:high]], axis=1)
        if high > length:
            return jnp.concatenate([ref[:, low:length], ref[:, 0 : high - length]], axis=1)
        return ref[:, low:high]

    every_lanes = 4
    for block in range(count):
        control[:, block * WIDE : (block + 1) * WIDE] = mm_parts(
            (window(high_s, block), window(low_s, block)), (lon1[0], lon1[1])
        )
        if block % every_lanes == every_lanes - 1:
            lanes = slice((block + 1 - every_lanes) * WIDE, (block + 1) * WIDE)
            outgoing.append(
                pltpu.make_async_copy(
                    control.at[:, lanes], control_h.at[:, lanes], out_sems.at[len(outgoing)]
                )
            )
            outgoing[-1].start()
    for copy in outgoing:
        copy.wait()


def _back_index(at, slots):
    return at + lax.div(at, slots) * (8 * LANES - slots)


def body(
    background_std,
    x_kernel,
    y_kernel,
    obs_owner,
    obs_cells,
    obs_weights,
    innovation,
    obs_precision,
    obs_counts,
):
    parts = lax.axis_size("pencil")
    levels = lax.axis_size("lev")
    me = lax.axis_index("pencil")
    _, columns, height = background_std.shape
    hold, stencil = obs_cells.shape
    margin = x_kernel.shape[1] // 2
    capacity = 2 * hold // parts
    senders = parts
    slots = senders * capacity
    rows_block = height // parts
    length = columns * parts
    blocks = height // LANES
    wide = columns + 2 * HALO
    group = min(GROUP, senders)
    chunks = senders // group
    layout = Layout(senders, hold, stencil, parts)
    std = background_std[0]

    packed = pl.pallas_call(
        functools.partial(
            pack_kernel, parts=parts, columns=columns, height=height, margin=margin
        ),
        out_shape=jax.ShapeDtypeStruct((parts, PACK, hold), F32),
        in_specs=[smem()] + [vmem()] * 5,
        out_specs=vmem(),
        compiler_params=params(),
        name="pack",
    )(
        obs_counts,
        obs_owner.T,
        obs_cells.T,
        obs_weights.T,
        innovation[None, :],
        obs_precision[None, :],
    )
    recv = lax.all_to_all(packed, "pencil", split_axis=0, concat_axis=0, tiled=True)

    right = [(p, (p + 1) % parts) for p in range(parts)]
    left = [(p, (p - 1) % parts) for p in range(parts)]
    std_l = lax.ppermute(std[columns - HALO :, :], "pencil", right)
    std_r = lax.ppermute(std[:HALO, :], "pencil", left)

    size = min(columns, WIDE)
    lat2, lon2, lat1, lon1 = pl.pallas_call(
        functools.partial(bands_kernel, rows_block=rows_block),
        out_shape=[
            jax.ShapeDtypeStruct((2, 3, 2 * WIDE, WIDE), BF),
            jax.ShapeDtypeStruct((2, size, size + 2 * HALO), BF),
            jax.ShapeDtypeStruct((2, rows_block, rows_block + 2 * PAD), BF),
            jax.ShapeDtypeStruct((2, 2 * WIDE, WIDE), BF),
        ],
        in_specs=[smem(), smem()],
        out_specs=[vmem()] * 4,
        compiler_params=params(),
        name="bands",
    )(x_kernel[0], y_kernel[0])

    meta = jnp.reshape(me, (1,)).astype(I32)
    ints, floats = pl.pallas_call(
        functools.partial(
            unpack_kernel,
            layout=layout,
            parts=parts,
            columns=columns,
            height=height,
            capacity=capacity,
            stencil=stencil,
            group=group,
        ),
        out_shape=[
            jax.ShapeDtypeStruct((layout.int_rows, LANES), I32),
            jax.ShapeDtypeStruct((layout.float_rows, LANES), F32),
        ],
        in_specs=[smem(), vmem()],
        out_specs=[vmem()] * 2,
        compiler_params=params(),
        name="unpack",
    )(meta, recv)
    ints = ints.reshape(-1)
    floats = floats.reshape(-1)

    acc = pltpu.VMEM((blocks * wide + 8, LANES), F32)
    column_slots = pltpu.VMEM((slots, LANES), F32)
    static = dict(
        layout=layout,
        columns=columns,
        height=height,
        hold=hold,
        stencil=stencil,
        capacity=capacity,
        senders=senders,
        parts=parts,
        levels=levels,
    )
    per = group * stencil * hold
    line = group * hold
    index_scratch = [
        pltpu.SMEM((per,), I32),
        pltpu.SMEM((per,), F32),
        pltpu.SMEM((group * layout.table,), I32),
    ]
    work = (
        [column_slots]
        + [pltpu.VMEM((wide, height), BF)] * 2
        + [
            pltpu.VMEM((columns, height), F32),
            pltpu.VMEM((HALO, height), F32),
            pltpu.VMEM((HALO, height), F32),
            pltpu.VMEM(lat2.shape, BF),
            pltpu.VMEM(lon2.shape, BF),
            pltpu.VMEM((columns, height), F32),
        ]
        + [acc] * COPIES
        + [
            pltpu.SemaphoreType.DMA((5,)),
            pltpu.SemaphoreType.DMA((5,)),
            pltpu.SemaphoreType.DMA((height // WIDE,)),
        ]
    )
    field_shape = jax.ShapeDtypeStruct((columns, height), F32)
    field0, message, factors, info = pl.pallas_call(
        functools.partial(apply_kernel, first=True, **static),
        out_shape=[
            field_shape,
            jax.ShapeDtypeStruct((parts, 8, LANES), F32),
            jax.ShapeDtypeStruct((stencil, slots), F32),
            jax.ShapeDtypeStruct((slots, LANES), F32),
        ],
        in_specs=[smem()] + [hbm()] * 7,
        out_specs=[hbm()] + [vmem()] * 3,
        scratch_shapes=index_scratch
        + [
            pltpu.SMEM((line,), F32),
            pltpu.SMEM((line,), F32),
            acc,
            column_slots,
            pltpu.VMEM((stencil * slots, LANES), F32),
        ]
        + work,
        compiler_params=params(),
        name="apply_first",
    )(meta, ints, floats, std, std_l, std_r, lat2, lon2)

    replies = lax.all_to_all(message, "pencil", split_axis=0, concat_axis=0, tiled=True)
    factors_all = lax.all_gather(factors, "pencil", axis=0)
    back = replies.reshape(-1)

    field1, sums = pl.pallas_call(
        functools.partial(apply_kernel, first=False, **static),
        out_shape=[
            field_shape,
            jax.ShapeDtypeStruct((parts * levels, 8, LANES), F32),
        ],
        in_specs=[smem()] + [hbm()] * 2 + [smem(), vmem(), vmem()] + [hbm()] * 5,
        out_specs=[hbm(), vmem()],
        scratch_shapes=index_scratch + work,
        compiler_params=params(),
        name="apply_second",
    )(meta, ints, floats, back, replies, info, std, std_l, std_r, lat2, lon2)

    totals = lax.all_to_all(sums, ("pencil", "lev"), split_axis=0, concat_axis=0, tiled=True)
    totals = totals.reshape(parts, levels, 8, LANES)

    by_chunk = factors_all.reshape(parts, stencil, chunks, group * capacity)
    by_chunk = jnp.transpose(by_chunk, (2, 0, 1, 3)).reshape(-1)
    high_rows = rows_block + 2 * PAD
    acc_rows = pltpu.VMEM(((length // LANES) * high_rows + 8, LANES), F32)
    control, increment = pl.pallas_call(
        functools.partial(
            final_kernel,
            layout=layout,
            hold=hold,
            stencil=stencil,
            capacity=capacity,
            senders=senders,
            parts=parts,
            length=length,
        ),
        out_shape=[
            jax.ShapeDtypeStruct((rows_block, length), F32),
            field_shape,
        ],
        in_specs=[hbm()] * 3 + [smem(), vmem()] + [hbm()] * 3 + [vmem()] * 2,
        out_specs=[hbm()] * 2,
        scratch_shapes=[
            pltpu.SMEM((per,), I32),
            pltpu.SMEM((line,), I32),
            pltpu.SMEM((group * layout.table,), I32),
            pltpu.SMEM((line,), I32),
            pltpu.SMEM((line,), I32),
            pltpu.SMEM((line,), F32),
            pltpu.SMEM((parts * stencil * group * capacity,), F32),
            pltpu.VMEM((columns, height), F32),
            pltpu.VMEM((columns, height), F32),
            pltpu.VMEM((columns, height), F32),
            pltpu.VMEM((rows_block, length), F32),
            pltpu.VMEM((rows_block, length), BF),
            pltpu.VMEM((rows_block, length), BF),
        ]
        + [acc_rows] * COPIES
        + [
            pltpu.SemaphoreType.DMA((7,)),
            pltpu.SemaphoreType.DMA((3,)),
            pltpu.SemaphoreType.DMA((1 + length // WIDE,)),
        ],
        compiler_params=params(),
        name="outputs",
    )(ints, floats, by_chunk, back, totals, std, field0, field1, lat1, lon1)
    return control[None], increment[None]


def solution(mesh):
    return jax.shard_map(
        body,
        mesh=mesh,
        in_specs=(
            P("lev", "pencil", None),
            P("lev", None),
            P("lev", None),
            P(("pencil", "lev"), None),
            P(("pencil", "lev"), None),
            P(("pencil", "lev"), None),
            P(("pencil", "lev")),
            P(("pencil", "lev")),
            P(("pencil", "lev")),
        ),
        out_specs=(P("lev", "pencil", None), P("lev", "pencil", None)),
        check_vma=False,
    )
```

time: 273 us -> 236 us (0.86); the launches traced: 271 us -> 239 us
  blocking collectives: 0 us -> 76.2 us
  Pallas kernels: 149 us -> 110 us
  waiting for transfers between devices: 22.2 us -> 1.93 us
  starting transfers between devices: 64.4 us -> 45.2 us
  local copies, waits for them, and re-layouts: 16.4 us -> 4.01 us
  other arithmetic: 9.28 us -> 0 us
  between operations: 9.31 us -> 1.54 us
    all_to_all x0 -> x1, blocking collectives: none -> 44.3 us  [body(): lax.all_to_all(message, 'pencil', split_axis=0, concat_axis=0, tiled=True)]
    all_gather x0 -> x1, blocking collectives: none -> 31.9 us  [body(): factors_all = lax.all_gather(factors, 'pencil', axis=0)]
    pallas_call x1, Pallas kernels: 62 us -> 36.1 us  [body(): pl.pallas_call(functools.partial(apply_kernel, first=True, **static), out...]
    all_to_all x3 -> x1, waiting for transfers between devices: 21.8 us -> 0.01 us  [body(): lax.all_to_all(sums, ('pencil', 'lev'), split_axis=0, concat_axis=0, tile...]
    all_to_all x3 -> x1, starting transfers between devices: 52.4 us -> 33.1 us  [body(): lax.all_to_all(sums, ('pencil', 'lev'), split_axis=0, concat_axis=0, tile...]
    pallas_call x1, Pallas kernels: 43.2 us -> 33.7 us  [body(): pl.pallas_call(functools.partial(apply_kernel, first=False, **static), ou...]
    unnamed x24 -> x11, local copies, waits for them, and re-layouts: 8.3 us -> 2.95 us
    broadcast_in_dim x3 -> x0, local copies, waits for them, and re-layouts: 3.56 us -> none  [the longest x2 1.98 us: total_of(): spread = jnp.broadcast_to(values[None], (parts * levels,) + values.shape)]
  transfers between devices with their start and end apart: 6 -> 4, of which waited for: 4 -> 1; matrix products, arithmetic and copies ran while one was open for 4% -> 1% of each run, Pallas kernels for 3% -> 4%
where the time goes in v2:
time: 236 us; the launch traced here: 239 us
  Pallas kernels  110 us (47%)
  blocking collectives  76.2 us (32%)
  starting transfers between devices  45.2 us (19%)
  local copies, waits for them, and re-layouts  4.01 us (2%)
    all_to_all x1, blocking collectives, body(): lax.all_to_all(message, 'pencil', split_axis=0, concat_axis=0, tiled=True)  44.3 us
    pallas_call x1, Pallas kernels, body(): pl.pallas_call(functools.partial(apply_kernel, first=True, **static), out...  36.1 us
    pallas_call x1, Pallas kernels, body(): pl.pallas_call(functools.partial(apply_kernel, first=False, **static), ou...  33.7 us
    all_to_all x1, starting transfers between devices, body(): lax.all_to_all(sums, ('pencil', 'lev'), split_axis=0, concat_axis=0, tile...  33.1 us
    all_gather x1, blocking collectives, body(): factors_all = lax.all_gather(factors, 'pencil', axis=0)  31.9 us
    pallas_call x1, Pallas kernels, body(): pl.pallas_call(functools.partial(final_kernel, layout=layout, hold=hold,...  27.9 us
    all_to_all x1, starting transfers between devices, body(): lax.all_to_all(packed, 'pencil', split_axis=0, concat_axis=0, tiled=True)  7.28 us
    pallas_call x1, Pallas kernels, body(): pl.pallas_call(functools.partial(bands_kernel, rows_block=rows_block), ou...  7.12 us
  transfers between devices with their start and end apart: 4, of which 1 were waited for; matrix products, arithmetic and copies ran while one was open for 1% of the time, Pallas kernels for 4%

profile of v2, /device:TPU:0, one launch (start us, length us, event | category | flops | bytes accessed | tf_op | source)
XLA Modules:
  0.0 239.0 jit_solution(6370691113996184278)
XLA Ops:
  1.3 3.3 %pack.1 = f32[8,40,256]{2,1,0:T(8,128)} custom-call(s32[1]{0:T(128)S(6)} %copy.12.counts, s32[1,256]{1,0:T(1,128)} %bitcast.37, s32[16,256]{1,0:T(8,128)} %bitcast.35, f32[16,256]{1,0:T(8,128)} %bitcast.36, f32[1,256]{1,0:T(1,128)} %bitcast.38, f32[1,256]{1,0:T(1,128)} %bitcast.39), custom_call_target="tpu_custom_call" | custom-call | tf_op jit(solution)/shard_map/pack/pallas_call | solution.py:841
  4.5 7.3 %all-to-all-start = ((f32[8,40,256]{2,1,0:T(8,128)}), f32[8,40,256]{2,1,0:T(8,128)S(1)}, u32[]{:S(2)}, u32[]{:S(2)}) async-start(f32[8,40,256]{2,1,0:T(8,128)} %pack.1), calls=%async_computation | async-start | bytes 655360 | tf_op jit(solution)/shard_map/all_to_all | solution.py:858
  11.8 1.1 slice_bitcast_fusion
  12.9 4.8 %collective-permute-start.1 = (f32[32,2048]{1,0:T(8,128)S(1)}, f32[32,2048]{1,0:T(8,128)S(1)}, u32[]{:S(2)}, u32[]{:S(2)}) collective-permute-start(f32[32,2048]{1,0:T(8,128)S(1)} %get-tuple-element.30), channel_id=1, source_target_pairs={{0,28},{4,0},{8,4},{12,8},{16,12},{20,16},{24,20},{28,24},{1,29},{... | collective-permute-start | bytes 786440 | tf_op jit(solution)/shard_map/ppermute | solution.py:863
  17.7 0.0 collective-permute-start
  17.7 7.1 %bands.1 = (bf16[2,3,512,256]{3,2,1,0:T(8,128)(2,1)}, bf16[2,256,320]{2,1,0:T(8,128)(2,1)}, bf16[2,256,288]{2,1,0:T(8,128)(2,1)}, bf16[2,512,256]{2,1,0:T(8,128)(2,1)}) custom-call(f32[31]{0:T(128)} %bitcast.42, f32[31]{0:T(128)} %bitcast.43), custom_call_target="tpu_custom_call" | custom-call | tf_op jit(solution)/shard_map/bands/pallas_call | solution.py:866
  24.8 0.0 all-to-all-done.recv
  24.8 0.0 copy-start
  24.8 0.7 copy-done
  25.5 2.0 unpack.1
  27.5 1.9 collective-permute-done.1.refs_5_.refs_8_
  29.4 0.0 copy-start.1
  29.4 0.0 collective-permute-done.refs_4_.refs_7_
  29.4 0.0 copy-start.2
  29.4 0.7 copy-done.1
  30.1 0.1 copy-done.2
  30.2 36.1 %apply_first.1 = (f32[512,2048]{1,0:T(8,128)}, f32[8,8,128]{2,1,0:T(8,128)}, f32[16,512]{1,0:T(8,128)}, f32[512,128]{1,0:T(8,128)}) custom-call(s32[1]{0:T(128)} %bitcast.meta.refs_0_, s32[77824]{0:T(1024)} %bitcast.24, f32[36864]{0:T(1024)} %bitcast.27, f32[512,2048]{1,0:T(8,128)} %bitcast.21, f32[32,2048]{1,0:T(8,128)} %copy-done.2, f32[32,2048]{1,0:T(8,128)} %copy-done.1, ...), custom_call_target="tpu_custom_call" | custom-call | tf_op jit(solution)/shard_map/apply_first/pallas_call | solution.py:943
  66.3 0.0 copy-start.4
  66.3 44.3 %all_to_all.15.refs_4_ = f32[8,8,128]{2,1,0:T(8,128)} all-to-all(f32[8,8,128]{2,1,0:T(8,128)} %get-tuple-element.21), channel_id=1, replica_groups=mesh['pencil'=8,'lev'=4] {'pencil'}, dimensions={0} | all-to-all | bytes 65536 | tf_op jit(solution)/shard_map/all_to_all | solution.py:966
  110.7 33.7 %apply_second.1 = (f32[512,2048]{1,0:T(8,128)}, f32[32,8,128]{2,1,0:T(8,128)}) custom-call(s32[1]{0:T(128)} %bitcast.meta.refs_0_, s32[77824]{0:T(1024)} %bitcast.25, f32[36864]{0:T(1024)} %bitcast.28, f32[8192]{0:T(1024)} %bitcast.32, f32[8,8,128]{2,1,0:T(8,128)} %all_to_all.15.refs_4_, f32[512,128]{1,0:T(8,128)} %get-tuple-element.22.refs_5_, ...), custom_call_target="tpu_custom_call" | custom-call | tf_op jit(solution)/shard_map/apply_second/pallas_call | solution.py:970
  144.4 33.1 %all-to-all-start.2 = ((f32[32,8,128]{2,1,0:T(8,128)}), f32[32,8,128]{2,1,0:T(8,128)S(1)}, u32[]{:S(2)}, u32[]{:S(2)}) async-start(f32[32,8,128]{2,1,0:T(8,128)} %get-tuple-element.23), calls=%async_computation.2 | async-start | bytes 262144 | tf_op jit(solution)/shard_map/all_to_all | solution.py:983
  177.6 0.0 copy-done.4
  177.6 31.9 %all-gather = f32[128,512]{1,0:T(8,128)S(1)} all-gather(f32[16,512]{1,0:T(8,128)S(1)} %copy-done.4), channel_id=2, replica_groups=mesh['pencil'=8,'lev'=4] {'pencil'}, dimensions={0}, use_global_device_ids=true | all-gather | bytes 294912 | tf_op jit(solution)/shard_map/all_gather | solution.py:967
  209.5 0.8 copy.11
  210.2 0.0 all-to-all-done.2
  210.2 0.0 copy-start.3
  210.2 0.7 copy-done.3
  210.9 27.9 %outputs.1 = (f32[256,4096]{1,0:T(8,128)}, f32[512,2048]{1,0:T(8,128)}) custom-call(s32[77824]{0:T(1024)} %bitcast.26, f32[36864]{0:T(1024)} %bitcast.29, f32[65536]{0:T(1024)} %bitcast.30, f32[8192]{0:T(1024)} %bitcast.33, f32[8,4,8,128]{3,2,1,0:T(8,128)} %bitcast.34, f32[512,2048]{1,0:T(8,128)} %bitcast.23, f32[512,2048]{1,0:T(8,128)} %get-tuple-element.24.field0_h, ...), custom_call_target="tpu_custom_call" | custom-call | tf_op jit(solution)/shard_map/outputs/pallas_call | solution.py:990
Async XLA Ops:
  4.5 20.2 %all-to-all-start = ((f32[8,40,256]{2,1,0:T(8,128)}), f32[8,40,256]{2,1,0:T(8,128)S(1)}, u32[]{:S(2)}, u32[]{:S(2)}) async-start(f32[8,40,256]{2,1,0:T(8,128)} %pack.1), calls=%async_computation | async-start | bytes 655360 | tf_op jit(solution)/shard_map/all_to_all | solution.py:858
  12.9 16.5 %collective-permute-start.1 = (f32[32,2048]{1,0:T(8,128)S(1)}, f32[32,2048]{1,0:T(8,128)S(1)}, u32[]{:S(2)}, u32[]{:S(2)}) collective-permute-start(f32[32,2048]{1,0:T(8,128)S(1)} %get-tuple-element.30), channel_id=1, source_target_pairs={{0,28},{4,0},{8,4},{12,8},{16,12},{20,16},{24,20},{28,24},{1,29},{... | collective-permute-start | bytes 786440 | tf_op jit(solution)/shard_map/ppermute | solution.py:863
  17.7 11.7 %collective-permute-start = (f32[32,2048]{1,0:T(8,128)S(1)}, f32[32,2048]{1,0:T(8,128)S(1)}, u32[]{:S(2)}, u32[]{:S(2)}) collective-permute-start(f32[32,2048]{1,0:T(8,128)S(1)} %get-tuple-element.31), channel_id=1, source_target_pairs={{0,4},{4,8},{8,12},{12,16},{16,20},{20,24},{24,28},{28,0},{1,5},{5... | collective-permute-start | bytes 786440 | tf_op jit(solution)/shard_map/ppermute | solution.py:862
  24.8 0.7 copy-start
  29.4 0.7 copy-start.1
  29.4 0.8 copy-start.2
  66.3 111.3 %copy-start.4 = (f32[16,512]{1,0:T(8,128)S(1)}, f32[16,512]{1,0:T(8,128)}, u32[]{:S(2)}) copy-start(f32[16,512]{1,0:T(8,128)} %get-tuple-element.20) | copy-start | bytes 98308
  144.4 65.8 %all-to-all-start.2 = ((f32[32,8,128]{2,1,0:T(8,128)}), f32[32,8,128]{2,1,0:T(8,128)S(1)}, u32[]{:S(2)}, u32[]{:S(2)}) async-start(f32[32,8,128]{2,1,0:T(8,128)} %get-tuple-element.23), calls=%async_computation.2 | async-start | bytes 262144 | tf_op jit(solution)/shard_map/all_to_all | solution.py:983
  210.2 0.7 copy-start.3
